TPU v7x, 512 devices: a whole 4x4x16 slice. The times are simulated.
512 devices in a mesh: seq: 64 (over y, z), head: 8 (over x, core).
Axes of the slice: x: 4, y: 4, z: 16, core: 2. Of those that a mesh axis runs over, the one named last changes fastest.
Arguments:
- queries: bfloat16 [65536, 4096], P('seq', 'head'), may hold values from -6 to 6
- keys: bfloat16 [65536, 4096], P('seq', 'head'), may hold values from -6 to 6
- values: bfloat16 [65536, 4096], P('seq', 'head'), may hold values from -6 to 6
- decay_rate: float32 [65536, 32], P('seq', 'head'), may hold values from 0 to 0.5
- gain: float32 [4096], replicated, may hold values from 0.25 to 1.75
Outputs:
- normed: bfloat16 [65536, 4096], P(('seq', 'head'))
All inputs are finite; a program needn't handle non-finite values. Where the computation divides by a largest or mean magnitude, that divisor is 1e-20 or more.
Results may differ from a plain program's by a relative error of at most 0.017.
Values may be sent and summed in bfloat16 or wider, within the bound.
No kernel may reach another device: no remote copies, remote signals or barrier semaphores. Data moves between devices by JAX's collectives and lax.ppermute only.
A program may use at most 64 MiB of HBM per device.

v0:
```python
import jax
import jax.numpy as jnp
from jax import lax
from jax.sharding import PartitionSpec as P


def per_device(queries, keys, values, decay_rate, gain):
    tok_count, feature_count = queries.shape
    head_count = decay_rate.shape[1]
    head_size = feature_count // head_count
    inverse_root = head_size ** (-0.5)
    query_grid = queries.reshape(tok_count, head_count, head_size)
    key_grid = keys.reshape(tok_count, head_count, head_size)
    value_grid = values.reshape(tok_count, head_count, head_size)
    decayed = -jnp.cumsum(decay_rate, axis=0)
    row_span = min(512, tok_count)
    positions = jnp.arange(tok_count)
    within_parts = []
    for row_start in range(0, tok_count, row_span):
        query_rows = query_grid[row_start : row_start + row_span]
        scores = jnp.einsum(
            "thd,shd->hts", query_rows, key_grid, preferred_element_type=jnp.float32
        )
        causal = positions[row_start : row_start + row_span, None] >= positions[None, :]
        spread = decayed[row_start : row_start + row_span].T[:, :, None] - decayed.T[:, None, :]
        decay_mat = jnp.exp(jnp.where(causal[None], spread, -jnp.inf))
        weight = (scores * decay_mat * inverse_root).astype(jnp.bfloat16)
        within_parts.append(
            jnp.einsum("hts,shd->thd", weight, value_grid, preferred_element_type=jnp.float32)
        )
    within = jnp.concatenate(within_parts, axis=0)
    last_row = decayed[-1]
    decayed_keys = (
        key_grid.astype(jnp.float32) * jnp.exp(last_row[None, :] - decayed)[:, :, None]
    ).astype(jnp.bfloat16)
    summary = jnp.einsum(
        "shd,she->hde", decayed_keys, value_grid, preferred_element_type=jnp.float32
    )
    scales = (jnp.max(jnp.abs(summary), axis=2) + 1e-06).astype(jnp.bfloat16)
    code_words = (summary / scales.astype(jnp.float32)[:, :, None]).astype(jnp.bfloat16)
    my_index = lax.axis_index("seq")
    all_last = lax.all_gather(last_row[None, :], "seq", axis=0, tiled=True)
    prefix_logs = jnp.cumsum(all_last, axis=0)
    before_mine = lax.dynamic_slice_in_dim(prefix_logs, jnp.maximum(my_index - 1, 0), 1, 0)[0]
    before_mine = jnp.where(my_index > 0, before_mine, 0.0)
    shard_codes = lax.all_gather(code_words[None], "seq", axis=0, tiled=True)
    shard_scales = lax.all_gather(scales[None], "seq", axis=0, tiled=True)
    shard_total = shard_codes.shape[0]
    shard_ids = jnp.arange(shard_total)
    factor = jnp.exp(jnp.minimum(before_mine[None, :] - prefix_logs, 0.0))
    factor = jnp.where((shard_ids < my_index)[:, None], factor, 0.0)
    restored = shard_codes.astype(jnp.float32) * shard_scales.astype(jnp.float32)[:, :, :, None]
    incoming_sum = jnp.sum(factor[:, :, None, None] * restored, axis=0)
    incoming = incoming_sum.astype(jnp.bfloat16)
    carried = jnp.einsum("thd,hde->the", query_grid, incoming, preferred_element_type=jnp.float32)
    carried = carried * (jnp.exp(decayed) * inverse_root)[:, :, None]
    retained = (within + carried).astype(jnp.bfloat16)
    owners = lax.axis_size("head")
    arranged = retained.reshape(owners, tok_count // owners, head_count, head_size)
    gain_grid = gain.reshape(-1, head_size)
    flat = lax.all_to_all(arranged, "head", split_axis=0, concat_axis=2, tiled=True).astype(
        jnp.float32
    )
    center = jnp.mean(flat, axis=3, keepdims=True)
    deviation = flat - center
    variance = jnp.mean(deviation * deviation, axis=3, keepdims=True)
    scaled = deviation / jnp.sqrt(variance + 1e-05) * gain_grid[None, None]
    normed = scaled.astype(jnp.bfloat16)
    return normed.reshape(tok_count // owners, -1)


def solution(mesh):
    placed = (P("seq", "head"), P("seq", "head"), P("seq", "head"), P("seq", "head"), P())
    return jax.shard_map(
        per_device, mesh=mesh, in_specs=placed, out_specs=P(("seq", "head"), None), check_vma=False
    )
```

profile of v0, /device:TPU:1, one launch (start us, length us, event | category | flops | bytes accessed | tf_op | source)
XLA Modules:
  0.0 230.1 jit_solution(7381952477574835219)
XLA Ops:
  6.5 0.0 copy-start
  6.5 0.0 copy-start.1
  6.5 0.0 all-gather.6.cloned.1.call-start
  6.5 0.9 copy.200
  7.4 1.1 reduce-window.6
  8.5 0.2 slice_reduce_fusion
  8.7 0.2 reduce-window.9
  8.9 0.1 negate_bitcast_fusion
  9.0 0.2 slice_reduce_fusion.1
  9.2 0.1 subtract_exponential_fusion
  9.2 1.5 copy.160
  10.7 0.0 copy-start.2
  10.8 0.0 copy-done
  10.8 1.5 abs_reduce_fusion
  12.4 0.8 copy.140
  13.1 0.0 all-gather.6.cloned.1.call-update
  13.2 70.2 %all-gather.2 = f32[64,1,4]{2,1,0:T(1,128)S(1)} all-gather(f32[1,1,4]{2,1,0:T(1,128)S(1)} %bitcast.127), channel_id=1, replica_groups=mesh['seq'=64,'head'=8] {'seq'}, dimensions={0}, use_global_device_ids=true | all-gather | bytes 1040 | tf_op jit(solution)/shard_map/all_gather | solution.py:42
  83.4 0.1 reduce_window_sum.25
  83.5 66.8 %all-gather.3 = bf16[64,4,128]{2,1,0:T(4,128)(2,1)S(1)} all-gather(bf16[1,4,128]{2,1,0:T(4,128)(2,1)S(1)} %get-tuple-element.13), channel_id=3, replica_groups=mesh['seq'=64,'head'=8] {'seq'}, dimensions={0}, use_global_device_ids=true | all-gather | bytes 66560 | tf_op jit(solution)/shard_map/all_gather | solution.py:47
  150.2 0.0 copy-done.2
  150.2 0.0 copy-done.1
  150.2 0.1 fusion.43
  150.3 1.0 copy.158
  151.4 1.0 copy.159
  152.4 0.1 exponential_select_fusion
  152.5 1.2 iota_compare_fusion.1
  153.7 1.2 iota_compare_fusion
  154.8 0.0 copy-start.3
  154.8 6.0 %fusion.17 = f32[512,4,128]{2,0,1:T(8,128)} fusion(bf16[1024,4,128]{0,2,1:T(8,128)(2,1)} %bitcast.112, f32[4,1024]{1,0:T(4,128)S(1)} %bitcast.121, f32[4,512]{1,0:T(4,128)S(1)} %get-tuple-element.9, pred[512,1024]{1,0:T(8,128)(4,1)} %iota_compare_fusion.1, bf16[512,4,128]{0,2,1:T(8,128)(2,1)} %bitcast.116, bf16[1024,512]{1,0:T(8,128)(2,1)S(1)} %copy-done), kind=kOutput, calls=%fused_computation.26 | convolution fusion | flops 1084227584 | bytes 4218880 | tf_op jit(solution)/shard_map/hts,shd->thd/dot_general | solution.py:29
  160.8 0.0 copy-done.3
  160.8 5.5 %fusion.16 = f32[512,4,128]{2,0,1:T(8,128)} fusion(bf16[1024,4,128]{0,2,1:T(8,128)(2,1)S(1)} %bitcast.113, f32[4,512]{1,0:T(4,128)S(1)} %get-tuple-element.10, f32[4,1024]{1,0:T(4,128)S(1)} %bitcast.122, pred[512,1024]{1,0:T(8,128)(4,1)} %iota_compare_fusion, bf16[512,4,128]{0,2,1:T(8,128)(2,1)} %bitcast.115, bf16[1024,512]{1,0:T(8,128)(2,1)S(1)} %copy-done), kind=kOutput, calls=%fused_computation.25 | convolution fusion | flops 1084227584 | bytes 4218880 | tf_op jit(solution)/shard_map/hts,shd->thd/dot_general | solution.py:29
  166.3 2.1 all-gather.6.cloned.1.call-done
  168.4 0.0 copy-start.5
  168.4 0.0 copy-start.6
  168.4 8.6 %fusion.1 = bf16[4,128,128]{2,1,0:T(8,128)(2,1)S(1)} fusion(bf16[64,4,128,128]{3,2,1,0:T(8,128)(2,1)} %bitcast.110, f32[64,4,128]{2,1,0:T(4,128)S(1)} %convert_element_type.105, f32[64,4]{1,0:T(8,128)S(1)} %exponential_select_fusion), kind=kLoop, calls=%fused_computation.2 | loop fusion | flops 16711680 | bytes 8651776 | tf_op jit(solution)/shard_map/reduce_sum | solution.py:53
  177.1 0.0 copy-done.5
  177.1 0.0 copy-done.6
  177.1 0.8 fusion.10
  177.9 0.0 copy-start.4
  177.9 0.1 copy.144
  178.0 42.0 %all_to_all.4 = bf16[8,128,4,128]{3,1,2,0:T(8,128)(2,1)S(1)} all-to-all(bf16[8,128,4,128]{3,1,2,0:T(8,128)(2,1)S(1)} %copy.144), channel_id=1, replica_groups=mesh['seq'=64,'head'=8] {'head'}, dimensions={0} | all-to-all | bytes 2097152 | tf_op jit(solution)/shard_map/all_to_all | solution.py:61
  220.0 0.7 copy.145
  220.6 0.2 bitcast_reduce_fusion
  220.9 0.3 fusion.15
  221.2 0.0 copy-done.4
  221.3 0.7 fusion.13
  222.0 1.3 copy.151
  (15 shorter events, 0.1 us)
Async XLA Ops:
  6.5 4.2 %copy-start = (bf16[1024,512]{1,0:T(8,128)(2,1)S(1)}, bf16[1024,512]{1,0:T(8,128)(2,1)}, u32[]{:S(2)}) copy-start(bf16[1024,512]{1,0:T(8,128)(2,1)} %param.6) | copy-start | bytes 3145732
  6.5 143.7 %copy-start.1 = (bf16[1024,512]{1,0:T(8,128)(2,1)S(1)}, bf16[1024,512]{1,0:T(8,128)(2,1)}, u32[]{:S(2)}) copy-start(bf16[1024,512]{1,0:T(8,128)(2,1)} %param.5) | copy-start | bytes 3145732
  6.5 161.9 %all-gather.6.cloned.1.call-start = ((), (), s32[]{:S(2)}) async-start(), calls=%async_computation.1 | async-start | bytes 8519680 | tf_op jit(solution)/shard_map/all_gather | solution.py:46
  10.7 139.5 %copy-start.2 = (bf16[1024,512]{0,1:T(8,128)(2,1)}, bf16[1024,512]{0,1:T(8,128)(2,1)S(1)}, u32[]{:S(2)}) copy-start(bf16[1024,512]{0,1:T(8,128)(2,1)S(1)} %copy.160) | copy-start | bytes 3145732
  154.8 6.0 %copy-start.3 = (bf16[1024,512]{0,1:T(8,128)(2,1)S(1)}, bf16[1024,512]{0,1:T(8,128)(2,1)}, u32[]{:S(2)}) copy-start(bf16[1024,512]{0,1:T(8,128)(2,1)} %copy-done.2) | copy-start | bytes 3145732
  168.4 8.6 %copy-start.5 = (f32[512,4,128]{2,0,1:T(8,128)S(1)}, f32[512,4,128]{2,0,1:T(8,128)}, u32[]{:S(2)}) copy-start(f32[512,4,128]{2,0,1:T(8,128)} %fusion.17) | copy-start | bytes 3145732
  168.4 8.6 %copy-start.6 = (f32[512,4,128]{2,0,1:T(8,128)S(1)}, f32[512,4,128]{2,0,1:T(8,128)}, u32[]{:S(2)}) copy-start(f32[512,4,128]{2,0,1:T(8,128)} %fusion.16) | copy-start | bytes 3145732
  177.9 43.4 %copy-start.4 = (f32[4096]{0:T(1024)S(1)}, f32[4096]{0:T(1024)}, u32[]{:S(2)}) copy-start(f32[4096]{0:T(1024)} %param.9) | copy-start | bytes 49156
Sparse Core Ops, SparseCore 0:
  13.3 155.1 all-gather.5
where the time goes:
time: 231 us; the launch traced here: 230 us
  blocking collectives  179 us (77%)
  other arithmetic  13.9 us (6%)
  matrix products  13.8 us (6%)
  between operations  13.6 us (6%)
  local copies, waits for them, and re-layouts  7.68 us (3%)
    all_gather x1, blocking collectives, per_device(): all_last = lax.all_gather(last_row[None, :], 'seq', axis=0, tiled=True)  70.2 us
    all_gather x1, blocking collectives, per_device(): shard_scales = lax.all_gather(scales[None], 'seq', axis=0, tiled=True)  66.8 us
    all_to_all x1, blocking collectives, per_device(): lax.all_to_all(arranged, 'head', split_axis=0, concat_axis=2, tiled=True)  42 us
    dot_general x2, matrix products, per_device(): jnp.einsum('hts,shd->thd', weight, value_grid, preferred_element_type=jnp...  11.5 us
    reduce_sum x1, other arithmetic, per_device(): incoming_sum = jnp.sum(factor[:, :, None, None] * restored, axis=0)  8.61 us
  transfers between devices with their start and end apart: 1, of which 1 were waited for; matrix products, arithmetic and copies ran while one was open for 7% of the time, Pallas kernels for 0%

commit v1 on v0

v1 whole, which is shorter than its diff:
```python
import functools

import jax
import jax.numpy as jnp
from jax import lax
from jax.experimental import pallas as pl
from jax.experimental.pallas import tpu as pltpu
from jax.sharding import PartitionSpec as P

LANE = 128
F32 = jnp.float32
BF16 = jnp.bfloat16
VMEM_BYTES = 48 * 1024 * 1024


def split_three(x):
    high = x.astype(BF16)
    rest = x - high.astype(F32)
    middle = rest.astype(BF16)
    low = (rest - middle.astype(F32)).astype(BF16)
    return high, middle, low


def chunk_sums(rate_row, after):
    tokens = rate_row.shape[1]
    count = tokens // LANE
    rows = jnp.concatenate([rate_row[:, n * LANE : (n + 1) * LANE] for n in range(count)], axis=0)
    source = lax.broadcasted_iota(jnp.int32, (LANE, LANE), 0)
    target = lax.broadcasted_iota(jnp.int32, (LANE, LANE), 1)
    picked = (source > target) if after else (source <= target)
    picked = jnp.where(picked, 1.0, 0.0).astype(BF16)
    sums = sum(jnp.dot(part, picked, preferred_element_type=F32) for part in split_three(rows))
    if after:
        totals = sums[:, :1] + rows[:, :1]
    else:
        totals = sums[:, LANE - 1 :]
    running = jnp.zeros((1, 1), F32)
    pieces = [None] * count
    for n in reversed(range(count)) if after else range(count):
        pieces[n] = sums[n : n + 1] + running
        running = running + totals[n : n + 1]
    return pieces, running


def summary_kernel(rate_ref, key_ref, value_ref, out_ref):
    head = pl.program_id(0)
    later, total = chunk_sums(rate_ref[pl.ds(head, 1), :], after=True)
    decay = jnp.exp(-jnp.concatenate(later, axis=1))
    key_t = key_ref[...].T
    decayed_keys = (key_t.astype(F32) * decay).astype(BF16)
    summary = jnp.dot(decayed_keys, value_ref[...], preferred_element_type=F32)
    size = summary.shape[0]
    scales = (jnp.max(jnp.abs(summary), axis=1, keepdims=True) + 1e-06).astype(BF16).astype(F32)
    codes = (summary / scales).astype(BF16)
    restored = (codes.astype(F32) * scales).astype(BF16)
    keep = jnp.broadcast_to(jnp.exp(-total), (1, LANE))
    parts = jnp.concatenate([p.astype(F32) for p in split_three(keep)] + [jnp.zeros((5, LANE), F32)], axis=0)
    parts = parts.astype(BF16)
    out_ref[:, :8, :] = restored.reshape(size // 8, 8, LANE)
    out_ref[:, 8:, :] = jnp.broadcast_to(parts[None], (size // 8, 8, LANE))


def scan_kernel(in_ref, out_ref):
    blocks = in_ref.shape[0]

    def step(i, state):
        out_ref[i] = state.astype(BF16)
        block = in_ref[i].astype(F32)
        keep = block[8:9] + block[9:10] + block[10:11]
        return state * keep + block[:8]

    lax.fori_loop(0, blocks, step, jnp.zeros((8, LANE), F32), unroll=4)


def within_kernel(inverse_root, span, rate_ref, query_ref, key_ref, value_ref, within_ref, query_out_ref):
    head = pl.program_id(0)
    tokens = query_ref.shape[0]
    upto, _ = chunk_sums(rate_ref[pl.ds(head, 1), :], after=False)
    count = len(upto)
    stacked = -jnp.concatenate(upto, axis=0)
    columns = jnp.concatenate([stacked] * (LANE // count), axis=0).T
    column = jnp.concatenate([columns[:, n : n + 1] for n in range(count)], axis=0)
    row = -jnp.concatenate(upto, axis=1)
    query = query_ref[...]
    query_out_ref[...] = (query.astype(F32) * (jnp.exp(column) * inverse_root)).astype(BF16)
    place_t = lax.broadcasted_iota(jnp.int32, (span, span), 0)
    place_s = lax.broadcasted_iota(jnp.int32, (span, span), 1)
    for i in range(tokens // span):
        at_t = slice(i * span, (i + 1) * span)
        total = jnp.zeros((span, query.shape[1]), F32)
        for j in range(i + 1):
            at_s = slice(j * span, (j + 1) * span)
            scores = lax.dot_general(
                query[at_t], key_ref[at_s, :], (((1,), (1,)), ((), ())), preferred_element_type=F32
            )
            spread = column[at_t] - row[:, at_s]
            if i == j:
                spread = jnp.where(place_t >= place_s, spread, -jnp.inf)
            weight = (scores * jnp.exp(spread) * inverse_root).astype(BF16)
            total += jnp.dot(weight, value_ref[at_s, :], preferred_element_type=F32)
        within_ref[at_t, :] = total


def finish_kernel(query_ref, within_ref, incoming_ref, gain_ref, out_ref):
    carried = jnp.dot(query_ref[...], incoming_ref[0], preferred_element_type=F32)
    retained = (within_ref[...] + carried).astype(BF16)
    size = retained.shape[1]
    ones = jnp.ones((size, size), BF16)
    center = jnp.dot(retained, ones, preferred_element_type=F32) * (1.0 / size)
    deviation = retained.astype(F32) - center
    square = deviation * deviation
    high = square.astype(BF16)
    low = (square - high.astype(F32)).astype(BF16)
    variance = jnp.dot(high, ones, preferred_element_type=F32) + jnp.dot(low, ones, preferred_element_type=F32)
    variance = variance * (1.0 / size)
    out_ref[...] = (deviation * lax.rsqrt(variance + 1e-05) * gain_ref[...]).astype(BF16)


def per_device(queries, keys, values, decay_rate, gain):
    tokens, features = queries.shape
    heads = decay_rate.shape[1]
    size = features // heads
    inverse_root = size ** (-0.5)
    blocks = lax.axis_size("seq")
    owners = lax.axis_size("head")
    rates = decay_rate.T
    params = pltpu.CompilerParams(vmem_limit_bytes=VMEM_BYTES)
    tall = pl.BlockSpec((tokens, size), lambda h: (0, h))
    whole_rates = pl.BlockSpec((heads, tokens), lambda h: (0, 0))
    state_rows = heads * size // blocks

    with jax.named_scope("summaries"):
        payload = pl.pallas_call(
            summary_kernel,
            grid=(heads,),
            in_specs=[whole_rates, tall, tall],
            out_specs=pl.BlockSpec((size // 8, 16, size), lambda h: (h, 0, 0)),
            out_shape=jax.ShapeDtypeStruct((blocks, 16, size), BF16),
            compiler_params=params,
            cost_estimate=pl.CostEstimate(flops=2 * heads * tokens * size * size, bytes_accessed=4 * tokens * features, transcendentals=0),
        )(rates, keys, values)
    gathered = lax.all_to_all(payload, "seq", 0, 0, tiled=True)
    with jax.named_scope("within"):
        within, scaled_queries = pl.pallas_call(
            functools.partial(within_kernel, inverse_root, 256),
            grid=(heads,),
            in_specs=[whole_rates, tall, tall, tall],
            out_specs=[tall, tall],
            out_shape=[
                jax.ShapeDtypeStruct((tokens, features), F32),
                jax.ShapeDtypeStruct((tokens, features), BF16),
            ],
            compiler_params=params,
            cost_estimate=pl.CostEstimate(
                flops=3 * heads * tokens * tokens * size, bytes_accessed=12 * tokens * features, transcendentals=heads * tokens * tokens
            ),
        )(rates, queries, keys, values)
    with jax.named_scope("block_scan"):
        before = pl.pallas_call(
            scan_kernel,
            out_shape=jax.ShapeDtypeStruct((blocks, 8, size), BF16),
            compiler_params=params,
        )(gathered)
    incoming = lax.all_to_all(before, "seq", 0, 0, tiled=True).reshape(heads, size, size)
    my_gain = lax.dynamic_slice_in_dim(gain, lax.axis_index("head") * features, features)[None]
    with jax.named_scope("finish"):
        normed = pl.pallas_call(
            finish_kernel,
            grid=(heads,),
            in_specs=[
                tall,
                tall,
                pl.BlockSpec((1, size, size), lambda h: (h, 0, 0)),
                pl.BlockSpec((1, size), lambda h: (0, h)),
            ],
            out_specs=tall,
            out_shape=jax.ShapeDtypeStruct((tokens, features), BF16),
            compiler_params=params,
        )(scaled_queries, within, incoming, my_gain)
    sent = normed.reshape(owners, tokens // owners, features)
    got = lax.all_to_all(sent, "head", 0, 0, tiled=True)
    return got.transpose(1, 0, 2).reshape(tokens // owners, owners * features)


def solution(mesh):
    placed = (P("seq", "head"), P("seq", "head"), P("seq", "head"), P("seq", "head"), P())
    return jax.shard_map(
        per_device, mesh=mesh, in_specs=placed, out_specs=P(("seq", "head"), None), check_vma=False
    )
```

time: 231 us -> 95.5 us (0.41)
  blocking collectives: 179 us -> 60.6 us
  Pallas kernels: 0 us -> 15.1 us
  other arithmetic: 13.9 us -> 0 us
  matrix products: 13.8 us -> 0 us
  between operations: 13.6 us -> 0.05 us
  starting transfers between devices: 0.01 us -> 7.59 us
    all_gather x2 -> x0, blocking collectives: 137 us -> none  [the longest x1 70.2 us: per_device(): all_last = lax.all_gather(last_row[None, :], 'seq', axis=0, tiled=True)]
    all_to_all x1 -> x2, blocking collectives: 42 us -> 60.6 us  [the longest x1 38.1 us: per_device(): gathered = lax.all_to_all(payload, 'seq', 0, 0, tiled=True)]
    pallas_call x0 -> x4, Pallas kernels: none -> 15.1 us  [the longest x1 8.14 us: per_device(): pl.pallas_call(functools.partial(within_kernel, inverse_root, 256), grid=...]
    dot_general x4 -> x0, matrix products: 13.8 us -> none  [the longest x2 11.5 us: per_device(): jnp.einsum('hts,shd->thd', weight, value_grid, preferred_element_type=jnp...]
    reduce_sum x3 -> x0, other arithmetic: 9.15 us -> none  [the longest x1 8.61 us: per_device(): incoming_sum = jnp.sum(factor[:, :, None, None] * restored, axis=0)]
    all_to_all x0 -> x1, starting transfers between devices: none -> 7.59 us  [per_device(): lax.all_to_all(before, 'seq', 0, 0, tiled=True).reshape(heads, size, size)]
    all_to_all x0 -> x1, waiting for transfers between devices: none -> 3.81 us  [per_device(): lax.all_to_all(before, 'seq', 0, 0, tiled=True).reshape(heads, size, size)]
    unnamed x18 -> x16, local copies, waits for them, and re-layouts: 2.95 us -> 5.99 us
  transfers between devices with their start and end apart: 1 -> 1, of which waited for: 1 -> 1; matrix products, arithmetic and copies ran while one was open for 7% -> 1% of each run, Pallas kernels for 0% -> 9%
where the time goes in v1:
time: 95.5 us; the launch traced here: 95 us
  blocking collectives  60.6 us (63%)
  Pallas kernels  15.1 us (16%)
  local copies, waits for them, and re-layouts  7.84 us (8%)
  starting transfers between devices  7.59 us (8%)
  waiting for transfers between devices  3.81 us (4%)
    all_to_all x1, blocking collectives, per_device(): gathered = lax.all_to_all(payload, 'seq', 0, 0, tiled=True)  38.1 us
    all_to_all x1, blocking collectives, per_device(): got = lax.all_to_all(sent, 'head', 0, 0, tiled=True)  22.5 us
    pallas_call x1, Pallas kernels, per_device(): pl.pallas_call(functools.partial(within_kernel, inverse_root, 256), grid=...  8.14 us
    all_to_all x1, starting transfers between devices, per_device(): lax.all_to_all(before, 'seq', 0, 0, tiled=True).reshape(heads, size, size)  7.59 us
    unnamed x16, local copies, waits for them, and re-layouts  5.99 us
    all_to_all x1, waiting for transfers between devices, per_device(): lax.all_to_all(before, 'seq', 0, 0, tiled=True).reshape(heads, size, size)  3.81 us
    pallas_call x1, Pallas kernels, per_device(): pl.pallas_call(finish_kernel, grid=(heads,), in_specs=[tall, tall, pl.Blo...  3.37 us
    pallas_call x1, Pallas kernels, per_device(): pl.pallas_call(summary_kernel, grid=(heads,), in_specs=[whole_rates, tall...  2.7 us
  transfers between devices with their start and end apart: 1, of which 1 were waited for; matrix products, arithmetic and copies ran while one was open for 1% of the time, Pallas kernels for 9%

profile of v1, /device:TPU:1, one launch (start us, length us, event | category | flops | bytes accessed | tf_op | source)
XLA Modules:
  0.0 95.0 jit_solution(15900882242763325495)
XLA Ops:
  0.0 0.0 copy-start.1
  0.0 1.2 %copy-done.1 = bf16[1024,512]{1,0:T(8,128)(2,1)S(1)} copy-done((bf16[1024,512]{1,0:T(8,128)(2,1)S(1)}, bf16[1024,512]{1,0:T(8,128)(2,1)}, u32[]{:S(2)}) %copy-start.1) | copy-done | bytes 1048600
  1.2 0.0 copy-start.3
  1.2 1.2 %copy-done.3 = bf16[1024,512]{1,0:T(8,128)(2,1)S(1)} copy-done((bf16[1024,512]{1,0:T(8,128)(2,1)S(1)}, bf16[1024,512]{1,0:T(8,128)(2,1)}, u32[]{:S(2)}) %copy-start.3) | copy-done | bytes 1048600
  2.5 0.0 copy-start.5
  2.5 0.7 copy-done.5
  3.2 0.0 copy-start.2
  3.2 0.0 copy-start.4
  3.2 0.0 copy-start.6
  3.2 2.7 %summaries.1 = bf16[64,16,128]{2,1,0:T(8,128)(2,1)S(1)} custom-call(f32[4,1024]{1,0:T(4,128)S(1)} %bitcast.9, bf16[1024,512]{1,0:T(8,128)(2,1)S(1)} %copy-done.1, bf16[1024,512]{1,0:T(8,128)(2,1)S(1)} %copy-done.3), custom_call_target="tpu_custom_call" | custom-call | flops 134217728 | bytes 2097152 | tf_op jit(solution)/shard_map/summaries/pallas_call | solution.py:133
  5.9 38.1 %all_to_all.15.in_ref = bf16[64,16,128]{2,1,0:T(8,128)(2,1)S(1)} all-to-all(bf16[64,16,128]{2,1,0:T(8,128)(2,1)S(1)} %summaries.1), channel_id=1, replica_groups=mesh['seq'=64,'head'=8] {'seq'}, dimensions={0} | all-to-all | bytes 524288 | tf_op jit(solution)/shard_map/all_to_all | solution.py:142
  44.0 0.9 block_scan.1
  44.9 7.6 %all-to-all-start.1 = ((bf16[64,8,128]{2,1,0:T(8,128)(2,1)}), bf16[64,8,128]{2,1,0:T(8,128)(2,1)S(1)}, u32[]{:S(2)}, u32[]{:S(2)}) async-start(bf16[64,8,128]{2,1,0:T(8,128)(2,1)} %block_scan.1), calls=%async_computation.1 | async-start | bytes 262144 | tf_op jit(solution)/shard_map/all_to_all | solution.py:164
  52.5 0.8 dynamic_slice.3
  53.3 0.0 copy-done.2
  53.3 0.0 copy-done.4
  53.3 0.0 copy-done.6
  53.3 0.0 copy-start.7
  53.3 1.2 %copy-done.7 = bf16[1024,512]{1,0:T(8,128)(2,1)S(1)} copy-done((bf16[1024,512]{1,0:T(8,128)(2,1)S(1)}, bf16[1024,512]{1,0:T(8,128)(2,1)}, u32[]{:S(2)}) %copy-start.7) | copy-done | bytes 1048600
  54.5 8.1 %within.1 = (f32[1024,512]{1,0:T(8,128)}, bf16[1024,512]{1,0:T(8,128)(2,1)S(1)}) custom-call(f32[4,1024]{1,0:T(4,128)S(1)} %bitcast.10, bf16[1024,512]{1,0:T(8,128)(2,1)S(1)} %copy-done.7, bf16[1024,512]{1,0:T(8,128)(2,1)S(1)} %copy-done.2, bf16[1024,512]{1,0:T(8,128)(2,1)S(1)} %copy-done.4), custom_call_target="tpu_custom_call" | custom-call | flops 1610612736 | bytes 6291456 | tf_op jit(solution)/shard_map/within/pallas_call | solution.py:144
  62.7 3.8 %all-to-all-done.1 = bf16[64,8,128]{2,1,0:T(8,128)(2,1)S(1)} async-done(((bf16[64,8,128]{2,1,0:T(8,128)(2,1)}), bf16[64,8,128]{2,1,0:T(8,128)(2,1)S(1)}, u32[]{:S(2)}, u32[]{:S(2)}) %all-to-all-start.1) | async-done | bytes 131104 | tf_op jit(solution)/shard_map/all_to_all | solution.py:164
  66.5 0.0 copy-start
  66.5 1.6 %copy-done = f32[1024,512]{1,0:T(8,128)S(1)} copy-done((f32[1024,512]{1,0:T(8,128)S(1)}, f32[1024,512]{1,0:T(8,128)}, u32[]{:S(2)}) %copy-start) | copy-done | bytes 2097176
  68.1 3.4 %finish.1 = bf16[1024,512]{1,0:T(8,128)(2,1)S(1)} custom-call(bf16[1024,512]{1,0:T(8,128)(2,1)S(1)} %get-tuple-element.7.query_ref, f32[1024,512]{1,0:T(8,128)S(1)} %copy-done, bf16[4,128,128]{2,1,0:T(8,128)(2,1)S(1)} %bitcast.8, f32[1,512]{1,0:T(1,128)S(1)} %bitcast.11), custom_call_target="tpu_custom_call" | custom-call | tf_op jit(solution)/shard_map/finish/pallas_call | solution.py:167
  71.4 22.5 %all_to_all.16 = bf16[8,128,512]{2,1,0:T(8,128)(2,1)S(1)} all-to-all(bf16[8,128,512]{2,1,0:T(8,128)(2,1)S(1)} %bitcast.7), channel_id=1, replica_groups=mesh['seq'=64,'head'=8] {'head'}, dimensions={0} | all-to-all | bytes 2097152 | tf_op jit(solution)/shard_map/all_to_all | solution.py:181
  93.9 1.1 %copy.7 = bf16[8,16,8,512]{3,2,0,1:T(8,128)(2,1)} copy(bf16[8,16,8,512]{3,2,1,0:T(8,128)(2,1)S(1)} %bitcast.12) | data formatting | bytes 2097152 | tf_op jit(solution)/shard_map/reshape | solution.py:182
Async XLA Ops:
  0.0 1.2 %copy-start.1 = (bf16[1024,512]{1,0:T(8,128)(2,1)S(1)}, bf16[1024,512]{1,0:T(8,128)(2,1)}, u32[]{:S(2)}) copy-start(bf16[1024,512]{1,0:T(8,128)(2,1)} %key_ref.3) | copy-start | bytes 3145732
  1.2 1.2 %copy-start.3 = (bf16[1024,512]{1,0:T(8,128)(2,1)S(1)}, bf16[1024,512]{1,0:T(8,128)(2,1)}, u32[]{:S(2)}) copy-start(bf16[1024,512]{1,0:T(8,128)(2,1)} %value_ref.3) | copy-start | bytes 3145732
  2.5 0.7 copy-start.5
  3.2 50.1 %copy-start.2 = (bf16[1024,512]{1,0:T(8,128)(2,1)S(1)}, bf16[1024,512]{1,0:T(8,128)(2,1)}, u32[]{:S(2)}) copy-start(bf16[1024,512]{1,0:T(8,128)(2,1)} %key_ref.3) | copy-start | bytes 3145732
  3.2 50.1 %copy-start.4 = (bf16[1024,512]{1,0:T(8,128)(2,1)S(1)}, bf16[1024,512]{1,0:T(8,128)(2,1)}, u32[]{:S(2)}) copy-start(bf16[1024,512]{1,0:T(8,128)(2,1)} %value_ref.3) | copy-start | bytes 3145732
  3.2 50.1 %copy-start.6 = (f32[1024,4]{0,1:T(4,128)S(1)}, f32[1024,4]{0,1:T(4,128)}, u32[]{:S(2)}) copy-start(f32[1024,4]{0,1:T(4,128)} %param.8) | copy-start | bytes 49156
  44.9 21.5 %all-to-all-start.1 = ((bf16[64,8,128]{2,1,0:T(8,128)(2,1)}), bf16[64,8,128]{2,1,0:T(8,128)(2,1)S(1)}, u32[]{:S(2)}, u32[]{:S(2)}) async-start(bf16[64,8,128]{2,1,0:T(8,128)(2,1)} %block_scan.1), calls=%async_computation.1 | async-start | bytes 262144 | tf_op jit(solution)/shard_map/all_to_all | solution.py:164
  53.3 1.2 %copy-start.7 = (bf16[1024,512]{1,0:T(8,128)(2,1)S(1)}, bf16[1024,512]{1,0:T(8,128)(2,1)}, u32[]{:S(2)}) copy-start(bf16[1024,512]{1,0:T(8,128)(2,1)} %query_ref.1) | copy-start | bytes 3145732
  66.5 1.6 %copy-start = (f32[1024,512]{1,0:T(8,128)S(1)}, f32[1024,512]{1,0:T(8,128)}, u32[]{:S(2)}) copy-start(f32[1024,512]{1,0:T(8,128)} %get-tuple-element.8.within_ref) | copy-start | bytes 6291460

commit v2 on v1

v2 whole, which is shorter than its diff:
```python
import functools
import math

import jax
import jax.numpy as jnp
from jax import lax
from jax.experimental import pallas as pl
from jax.experimental.pallas import tpu as pltpu
from jax.sharding import PartitionSpec as P

LANE = 128
F32 = jnp.float32
BF16 = jnp.bfloat16
SLOT = 10
LOG2_E = 1.4426950408889634
SMALL_VMEM = 16 * 1024 * 1024
LARGE_VMEM = 40 * 1024 * 1024


def split_three(x):
    high = x.astype(BF16)
    rest = x - high.astype(F32)
    middle = rest.astype(BF16)
    low = (rest - middle.astype(F32)).astype(BF16)
    return high, middle, low


def chunk_sums(rates, after):
    heads, tokens = rates.shape
    count = tokens // LANE
    rows = jnp.concatenate([rates[:, n * LANE : (n + 1) * LANE] for n in range(count)], axis=0)
    source = lax.broadcasted_iota(jnp.int32, (LANE, LANE), 0)
    target = lax.broadcasted_iota(jnp.int32, (LANE, LANE), 1)
    picked = (source > target) if after else (source <= target)
    picked = jnp.where(picked, 1.0, 0.0).astype(BF16)
    sums = sum(jnp.dot(part, picked, preferred_element_type=F32) for part in split_three(rows))
    if after:
        totals = sums[:, :1] + rows[:, :1]
    else:
        totals = sums[:, LANE - 1 :]
    running = jnp.zeros((heads, 1), F32)
    pieces = [None] * count
    for n in reversed(range(count)) if after else range(count):
        at = slice(n * heads, (n + 1) * heads)
        pieces[n] = sums[at] + running
        running = running + totals[at]
    return pieces, running


def summary_kernel(rate_hbm, key_hbm, value_hbm, out_ref, rates_ref, key_ref, value_ref, sems):
    heads, tokens = rates_ref.shape
    size = key_ref.shape[1] // heads
    copies = [
        pltpu.make_async_copy(source, target, sems.at[n])
        for n, (source, target) in enumerate(
            ((rate_hbm, rates_ref), (key_hbm, key_ref), (value_hbm, value_ref))
        )
    ]
    for copy in copies:
        copy.start()
    copies[0].wait()
    later, totals = chunk_sums(rates_ref[...], after=True)
    decays = jnp.exp(-jnp.concatenate(later, axis=1))
    keeps = jnp.exp(-totals)
    copies[1].wait()
    decayed_keys = []
    for h in range(heads):
        key_t = key_ref[:, h * size : (h + 1) * size].T
        decayed_keys.append((key_t.astype(F32) * decays[h : h + 1]).astype(BF16))
    copies[2].wait()
    for h in range(heads):
        summary = jnp.dot(decayed_keys[h], value_ref[:, h * size : (h + 1) * size], preferred_element_type=F32)
        scales = (jnp.max(jnp.abs(summary), axis=1, keepdims=True) + 1e-06).astype(BF16).astype(F32)
        codes = (summary / scales).astype(BF16)
        restored = codes.astype(F32) * scales
        keep = jnp.broadcast_to(keeps[h : h + 1], (1, LANE))
        parts = [p.astype(F32) for p in split_three(keep)[:2]]
        rows = []
        for i in range(size // 8):
            rows += [restored[i * 8 : (i + 1) * 8]] + parts
        filled = size // 8 * SLOT
        out_ref[h * filled : (h + 1) * filled, :] = jnp.concatenate(rows, axis=0).astype(BF16)


def scan_kernel(in_ref, out_ref):
    blocks = out_ref.shape[0]
    state = jnp.zeros((8, LANE), F32)
    for first in range(0, blocks, 8):
        rows = in_ref[first * SLOT : (first + 8) * SLOT, :].astype(F32)
        states = []
        for i in range(8):
            states.append(state)
            slot = rows[i * SLOT : (i + 1) * SLOT]
            state = state * (slot[8:9] + slot[9:10]) + slot[:8]
        out_ref[first : first + 8] = jnp.stack(states).astype(BF16)


def within_kernel(
    span,
    head_group_ref,
    gain_ref,
    rate_hbm,
    query_hbm,
    key_hbm,
    value_hbm,
    parts_ref,
    gain_out_ref,
    rates_ref,
    inputs_ref,
    total_ref,
    sems,
):
    heads, tokens = rates_ref.shape
    size = inputs_ref.shape[3]
    rate_copy = pltpu.make_async_copy(rate_hbm, rates_ref, sems.at[0])
    rate_copy.start()
    copies = []
    for h in range(heads):
        for n, source in enumerate((query_hbm, key_hbm, value_hbm)):
            copy = pltpu.make_async_copy(
                source.at[:, pl.ds(h * size, size)], inputs_ref.at[h, n], sems.at[1 + 3 * h + n]
            )
            copy.start()
            copies.append(copy)
    for h in range(heads):
        gain_out_ref[h : h + 1] = gain_ref[pl.ds(head_group_ref[0] * heads + h, 1), :]
    rate_copy.wait()
    upto, _ = chunk_sums(rates_ref[...], after=False)
    count = len(upto)
    stacked = -jnp.concatenate(upto, axis=0) * LOG2_E
    columns = jnp.concatenate([stacked] * (LANE // (count * heads)), axis=0).T
    place_t = lax.broadcasted_iota(jnp.int32, (span, span), 0)
    place_s = lax.broadcasted_iota(jnp.int32, (span, span), 1)
    for h in range(heads):
        for copy in copies[3 * h : 3 * h + 3]:
            copy.wait()
        at_h = slice(h * size, (h + 1) * size)
        places = [n * heads + h for n in range(count)]
        column = jnp.concatenate([columns[:, n : n + 1] for n in places], axis=0) - 0.5 * math.log2(size)
        row = jnp.concatenate([stacked[n : n + 1] for n in places], axis=1)
        parts_ref[0, :, at_h] = (inputs_ref[h, 0].astype(F32) * jnp.exp2(column)).astype(BF16)
        for first in range(0, tokens, span):
            at_s = slice(first, first + span)
            scores = lax.dot_general(
                inputs_ref[h, 0, first:, :],
                inputs_ref[h, 1, at_s, :],
                (((1,), (1,)), ((), ())),
                preferred_element_type=F32,
            )
            weights = []
            for start in range(first, tokens, span):
                spread = column[start : start + span] - row[:, at_s]
                if start == first:
                    spread = jnp.where(place_t >= place_s, spread, -jnp.inf)
                weights.append((scores[start - first : start - first + span] * jnp.exp2(spread)).astype(BF16))
            part = jnp.dot(jnp.concatenate(weights, axis=0), inputs_ref[h, 2, at_s, :], preferred_element_type=F32)
            if first == 0:
                total_ref[...] = part
            else:
                total_ref[first:, :] += part
        parts_ref[1, :, at_h] = total_ref[...].astype(BF16)


def finish_kernel(span, parts_ref, incoming_ref, gain_ref, out_ref):
    tokens = parts_ref.shape[1]
    heads, size, _ = incoming_ref.shape
    mean_of = jnp.full((size, size), 1.0 / size, BF16)
    for h in range(heads):
        columns = slice(h * size, (h + 1) * size)
        gain = gain_ref[h : h + 1]
        for first in range(0, tokens, span):
            at = slice(first, first + span)
            carried = jnp.dot(parts_ref[0, at, columns], incoming_ref[h], preferred_element_type=F32)
            retained = (parts_ref[1, at, columns].astype(F32) + carried).astype(BF16)
            center = jnp.dot(retained, mean_of, preferred_element_type=F32)
            deviation = retained.astype(F32) - center
            variance = jnp.sum(deviation * deviation, axis=1, keepdims=True) * (1.0 / size)
            out_ref[at, columns] = (deviation * lax.rsqrt(variance + 1e-05) * gain).astype(BF16)


def per_device(queries, keys, values, decay_rate, gain):
    tokens, features = queries.shape
    heads = decay_rate.shape[1]
    size = features // heads
    blocks = lax.axis_size("seq")
    owners = lax.axis_size("head")
    rates = decay_rate.T
    params = pltpu.CompilerParams(vmem_limit_bytes=SMALL_VMEM)

    in_hbm = pl.BlockSpec(memory_space=pl.ANY)
    in_vmem = pl.BlockSpec(memory_space=pltpu.VMEM)
    in_smem = pl.BlockSpec(memory_space=pltpu.SMEM)
    head_group = lax.axis_index("head").astype(jnp.int32).reshape(1)

    with jax.named_scope("summaries"):
        payload = pl.pallas_call(
            summary_kernel,
            in_specs=[in_hbm] * 3,
            out_specs=in_vmem,
            out_shape=jax.ShapeDtypeStruct((blocks * SLOT, size), BF16),
            scratch_shapes=[
                pltpu.VMEM((heads, tokens), F32),
                pltpu.VMEM((tokens, features), BF16),
                pltpu.VMEM((tokens, features), BF16),
                pltpu.SemaphoreType.DMA((3,)),
            ],
            cost_estimate=pl.CostEstimate(flops=2 * heads * tokens * size * size, bytes_accessed=4 * tokens * features, transcendentals=0),
        )(rates, keys, values)
    slots = payload.reshape(blocks, SLOT // 2, 2, size)
    gathered = lax.all_to_all(slots, "seq", 0, 0, tiled=True).reshape(blocks * SLOT, size)
    with jax.named_scope("within"):
        parts, my_gain = pl.pallas_call(
            functools.partial(within_kernel, 256),
            in_specs=[in_smem, in_vmem] + [in_hbm] * 4,
            out_specs=[in_vmem] * 2,
            out_shape=[
                jax.ShapeDtypeStruct((2, tokens, features), BF16),
                jax.ShapeDtypeStruct((heads, size), F32),
            ],
            scratch_shapes=[
                pltpu.VMEM((heads, tokens), F32),
                pltpu.VMEM((heads, 3, tokens, size), BF16),
                pltpu.VMEM((tokens, size), F32),
                pltpu.SemaphoreType.DMA((1 + 3 * heads,)),
            ],
            compiler_params=pltpu.CompilerParams(vmem_limit_bytes=LARGE_VMEM),
            cost_estimate=pl.CostEstimate(
                flops=3 * heads * tokens * tokens * size, bytes_accessed=12 * tokens * features, transcendentals=heads * tokens * tokens
            ),
        )(head_group, gain.reshape(-1, size), rates, queries, keys, values)
    gathered, parts, my_gain = lax.optimization_barrier((gathered, parts, my_gain))
    with jax.named_scope("block_scan"):
        before = pl.pallas_call(
            scan_kernel,
            in_specs=[in_vmem],
            out_specs=in_vmem,
            out_shape=jax.ShapeDtypeStruct((blocks, 8, size), BF16),
            compiler_params=params,
        )(gathered)
    incoming = lax.all_to_all(before, "seq", 0, 0, tiled=True).reshape(heads, size, size)
    with jax.named_scope("finish"):
        normed = pl.pallas_call(
            functools.partial(finish_kernel, 256),
            in_specs=[in_vmem] * 3,
            out_specs=in_vmem,
            out_shape=jax.ShapeDtypeStruct((tokens, features), BF16),
            compiler_params=params,
        )(parts, incoming, my_gain)
    sent = normed.reshape(owners, tokens // owners, features)
    got = lax.all_to_all(sent, "head", 0, 0, tiled=True)
    return got.transpose(1, 0, 2).reshape(tokens // owners, owners * features)


def solution(mesh):
    placed = (P("seq", "head"), P("seq", "head"), P("seq", "head"), P("seq", "head"), P())
    return jax.shard_map(
        per_device, mesh=mesh, in_specs=placed, out_specs=P(("seq", "head"), None), check_vma=False
    )
```

time: 95.5 us -> 83.8 us (0.88)
  blocking collectives: 60.6 us -> 43.8 us
  starting transfers between devices: 7.59 us -> 19.3 us
  Pallas kernels: 15.1 us -> 9.2 us
  local copies, waits for them, and re-layouts: 7.84 us -> 3.54 us
  waiting for transfers between devices: 3.81 us -> 7.56 us
    all_to_all x1, blocking collectives: 38.1 us -> 21.3 us  [per_device(): lax.all_to_all(before, 'seq', 0, 0, tiled=True).reshape(heads, size, size)]
    all_to_all x1, starting transfers between devices: 7.59 us -> 19.3 us  [per_device(): lax.all_to_all(slots, 'seq', 0, 0, tiled=True).reshape(blocks * SLOT, size)]
    pallas_call x4, Pallas kernels: 15.1 us -> 9.2 us  [the longest x1 5.04 us: per_device(): pl.pallas_call(functools.partial(within_kernel, 256), in_specs=[in_smem,...]
    all_to_all x1, waiting for transfers between devices: 3.81 us -> 7.56 us  [per_device(): lax.all_to_all(slots, 'seq', 0, 0, tiled=True).reshape(blocks * SLOT, size)]
    unnamed x16 -> x10, local copies, waits for them, and re-layouts: 5.99 us -> 2.46 us
  transfers between devices with their start and end apart: 1 -> 1, of which waited for: 1 -> 1; matrix products, arithmetic and copies ran while one was open for 1% -> 0% of each run, Pallas kernels for 9% -> 6%
where the time goes in v2:
time: 83.8 us; the launch traced here: 83.5 us
  blocking collectives  43.8 us (52%)
  starting transfers between devices  19.3 us (23%)
  Pallas kernels  9.2 us (11%)
  waiting for transfers between devices  7.56 us (9%)
  local copies, waits for them, and re-layouts  3.54 us (4%)
    all_to_all x1, blocking collectives, per_device(): got = lax.all_to_all(sent, 'head', 0, 0, tiled=True)  22.5 us
    all_to_all x1, blocking collectives, per_device(): lax.all_to_all(before, 'seq', 0, 0, tiled=True).reshape(heads, size, size)  21.3 us
    all_to_all x1, starting transfers between devices, per_device(): lax.all_to_all(slots, 'seq', 0, 0, tiled=True).reshape(blocks * SLOT, size)  19.3 us
    all_to_all x1, waiting for transfers between devices, per_device(): lax.all_to_all(slots, 'seq', 0, 0, tiled=True).reshape(blocks * SLOT, size)  7.56 us
    pallas_call x1, Pallas kernels, per_device(): pl.pallas_call(functools.partial(within_kernel, 256), in_specs=[in_smem,...  5.04 us
    pallas_call x1, Pallas kernels, per_device(): pl.pallas_call(summary_kernel, in_specs=[in_hbm] * 3, out_specs=in_vmem,...  2.96 us
    unnamed x10, local copies, waits for them, and re-layouts  2.46 us
  transfers between devices with their start and end apart: 1, of which 1 were waited for; matrix products, arithmetic and copies ran while one was open for 0% of the time, Pallas kernels for 6%

profile of v2, /device:TPU:1, one launch (start us, length us, event | category | flops | bytes accessed | tf_op | source)
XLA Modules:
  0.0 83.5 jit_solution(15366540397639802659)
XLA Ops:
  0.0 0.0 copy-start
  0.0 0.0 copy-start.2
  0.0 0.0 copy-start.4
  0.0 3.0 %summaries.1 = bf16[640,128]{1,0:T(8,128)(2,1)} custom-call(f32[4,1024]{1,0:T(4,128)} %bitcast.13, bf16[1024,512]{1,0:T(8,128)(2,1)} %key_hbm.3, bf16[1024,512]{1,0:T(8,128)(2,1)} %value_hbm.3), custom_call_target="tpu_custom_call" | custom-call | flops 134217728 | bytes 2097152 | tf_op jit(solution)/shard_map/summaries/pallas_call | solution.py:196
  3.0 19.3 %all-to-all-start = ((bf16[64,5,2,128]{3,2,1,0:T(2,128)(2,1)}), bf16[64,5,2,128]{3,2,1,0:T(2,128)(2,1)S(1)}, u32[]{:S(2)}, u32[]{:S(2)}) async-start(bf16[64,5,2,128]{3,2,1,0:T(2,128)(2,1)} %bitcast.17), calls=%async_computation | async-start | bytes 327680 | tf_op jit(solution)/shard_map/all_to_all | solution.py:210
  22.3 0.0 copy-done
  22.3 0.0 copy-done.2
  22.3 0.0 copy-done.4
  22.3 0.0 copy-start.1
  22.3 1.2 %copy-done.1 = bf16[1024,512]{1,0:T(8,128)(2,1)S(1)} copy-done((bf16[1024,512]{1,0:T(8,128)(2,1)S(1)}, bf16[1024,512]{1,0:T(8,128)(2,1)}, u32[]{:S(2)}) %copy-start.1) | copy-done | bytes 1048600
  23.5 0.0 copy-start.3
  23.5 1.2 %copy-done.3 = bf16[1024,512]{1,0:T(8,128)(2,1)S(1)} copy-done((bf16[1024,512]{1,0:T(8,128)(2,1)S(1)}, bf16[1024,512]{1,0:T(8,128)(2,1)}, u32[]{:S(2)}) %copy-start.3) | copy-done | bytes 1048600
  24.8 5.0 %within.1 = (bf16[2,1024,512]{2,1,0:T(8,128)(2,1)S(1)}, f32[4,128]{1,0:T(4,128)S(1)}) custom-call(s32[1]{0:T(128)} %bitcast.3.head_group_ref, f32[32,128]{1,0:T(8,128)S(1)} %bitcast.15, f32[4,1024]{1,0:T(4,128)S(1)} %bitcast.14, bf16[1024,512]{1,0:T(8,128)(2,1)S(1)} %copy-done.3, bf16[1024,512]{1,0:T(8,128)(2,1)S(1)} %copy-done, bf16[1024,512]{1,0:T(8,128)(2,1)S(1)} %copy-done.1), custom_call_target="tpu_custom_call" | custom-call | flops 1610612736 | bytes 6291456 | tf_op jit(solution)/shard_map/within/pallas_call | solution.py:212
  29.8 7.6 %all-to-all-done = bf16[64,5,2,128]{3,2,1,0:T(2,128)(2,1)S(1)} async-done(((bf16[64,5,2,128]{3,2,1,0:T(2,128)(2,1)}), bf16[64,5,2,128]{3,2,1,0:T(2,128)(2,1)S(1)}, u32[]{:S(2)}, u32[]{:S(2)}) %all-to-all-start) | async-done | bytes 163872 | tf_op jit(solution)/shard_map/all_to_all | solution.py:210
  37.4 0.1 block_scan.1
  37.5 21.3 %all_to_all.15 = bf16[64,8,128]{2,1,0:T(8,128)(2,1)S(1)} all-to-all(bf16[64,8,128]{2,1,0:T(8,128)(2,1)S(1)} %block_scan.1), channel_id=1, replica_groups=mesh['seq'=64,'head'=8] {'seq'}, dimensions={0} | all-to-all | bytes 262144 | tf_op jit(solution)/shard_map/all_to_all | solution.py:240
  58.8 1.1 %finish.1 = bf16[1024,512]{1,0:T(8,128)(2,1)S(1)} custom-call(bf16[2,1024,512]{2,1,0:T(8,128)(2,1)S(1)} %get-tuple-element.12.parts_ref, bf16[4,128,128]{2,1,0:T(8,128)(2,1)S(1)} %bitcast.12, f32[4,128]{1,0:T(4,128)S(1)} %get-tuple-element.14.gain_ref), custom_call_target="tpu_custom_call" | custom-call | tf_op jit(solution)/shard_map/finish/pallas_call | solution.py:242
  59.9 22.5 %all_to_all.16 = bf16[8,128,512]{2,1,0:T(8,128)(2,1)S(1)} all-to-all(bf16[8,128,512]{2,1,0:T(8,128)(2,1)S(1)} %bitcast.10), channel_id=1, replica_groups=mesh['seq'=64,'head'=8] {'head'}, dimensions={0} | all-to-all | bytes 2097152 | tf_op jit(solution)/shard_map/all_to_all | solution.py:250
  82.4 1.1 %copy.7 = bf16[8,16,8,512]{3,2,0,1:T(8,128)(2,1)} copy(bf16[8,16,8,512]{3,2,1,0:T(8,128)(2,1)S(1)} %bitcast.16) | data formatting | bytes 2097152 | tf_op jit(solution)/shard_map/reshape | solution.py:251
Async XLA Ops:
  0.0 22.3 %copy-start = (bf16[1024,512]{1,0:T(8,128)(2,1)S(1)}, bf16[1024,512]{1,0:T(8,128)(2,1)}, u32[]{:S(2)}) copy-start(bf16[1024,512]{1,0:T(8,128)(2,1)} %key_hbm.3) | copy-start | bytes 3145732
  0.0 22.3 %copy-start.2 = (f32[1024,4]{0,1:T(4,128)S(1)}, f32[1024,4]{0,1:T(4,128)}, u32[]{:S(2)}) copy-start(f32[1024,4]{0,1:T(4,128)} %param.8) | copy-start | bytes 49156
  0.0 22.3 %copy-start.4 = (f32[4096]{0:T(1024)S(1)}, f32[4096]{0:T(1024)}, u32[]{:S(2)}) copy-start(f32[4096]{0:T(1024)} %param.9) | copy-start | bytes 49156
  3.0 34.4 %all-to-all-start = ((bf16[64,5,2,128]{3,2,1,0:T(2,128)(2,1)}), bf16[64,5,2,128]{3,2,1,0:T(2,128)(2,1)S(1)}, u32[]{:S(2)}, u32[]{:S(2)}) async-start(bf16[64,5,2,128]{3,2,1,0:T(2,128)(2,1)} %bitcast.17), calls=%async_computation | async-start | bytes 327680 | tf_op jit(solution)/shard_map/all_to_all | solution.py:210
  22.3 1.2 %copy-start.1 = (bf16[1024,512]{1,0:T(8,128)(2,1)S(1)}, bf16[1024,512]{1,0:T(8,128)(2,1)}, u32[]{:S(2)}) copy-start(bf16[1024,512]{1,0:T(8,128)(2,1)} %value_hbm.3) | copy-start | bytes 3145732
  23.5 1.2 %copy-start.3 = (bf16[1024,512]{1,0:T(8,128)(2,1)S(1)}, bf16[1024,512]{1,0:T(8,128)(2,1)}, u32[]{:S(2)}) copy-start(bf16[1024,512]{1,0:T(8,128)(2,1)} %query_hbm.1) | copy-start | bytes 3145732

commit v3 on v2

--- a/solution.py
+++ b/solution.py
@@ -12,6 +12,8 @@
 F32 = jnp.float32
 BF16 = jnp.bfloat16
 SLOT = 10
+FIRST_SEQ = 41
+FIRST_HEAD = 4
 LOG2_E = 1.4426950408889634
 SMALL_VMEM = 16 * 1024 * 1024
 LARGE_VMEM = 40 * 1024 * 1024
@@ -75,56 +77,43 @@
         restored = codes.astype(F32) * scales
         keep = jnp.broadcast_to(keeps[h : h + 1], (1, LANE))
         parts = [p.astype(F32) for p in split_three(keep)[:2]]
-        rows = []
-        for i in range(size // 8):
-            rows += [restored[i * 8 : (i + 1) * 8]] + parts
-        filled = size // 8 * SLOT
-        out_ref[h * filled : (h + 1) * filled, :] = jnp.concatenate(rows, axis=0).astype(BF16)
-
-
-def scan_kernel(in_ref, out_ref):
-    blocks = out_ref.shape[0]
+        chunks = size // 8
+        for start in range(0, chunks, 8):
+            rows = []
+            for i in range(start, start + 8):
+                rows += [restored[i * 8 : (i + 1) * 8]] + parts
+            slot = h * chunks + start
+            out_ref[slot * SLOT : (slot + 8) * SLOT, :] = jnp.concatenate(rows, axis=0).astype(BF16)
+
+
+def scan_kernel(order, in_ref, out_ref):
     state = jnp.zeros((8, LANE), F32)
-    for first in range(0, blocks, 8):
-        rows = in_ref[first * SLOT : (first + 8) * SLOT, :].astype(F32)
-        states = []
-        for i in range(8):
-            states.append(state)
-            slot = rows[i * SLOT : (i + 1) * SLOT]
-            state = state * (slot[8:9] + slot[9:10]) + slot[:8]
-        out_ref[first : first + 8] = jnp.stack(states).astype(BF16)
+    groups = [in_ref[n * SLOT : (n + 8) * SLOT, :].astype(F32) for n in range(0, len(order), 8)]
+    for block in range(len(order)):
+        slot = order.index(block)
+        out_ref[slot] = state.astype(BF16)
+        rows = groups[slot // 8]
+        at = slot % 8 * SLOT
+        keep = rows[at + 8 : at + 9] + rows[at + 9 : at + 10]
+        state = state * keep + rows[at : at + 8]
 
 
 def within_kernel(
     span,
     head_group_ref,
     gain_ref,
-    rate_hbm,
-    query_hbm,
-    key_hbm,
-    value_hbm,
+    rates_ref,
+    query_ref,
+    key_ref,
+    value_ref,
     parts_ref,
     gain_out_ref,
-    rates_ref,
-    inputs_ref,
     total_ref,
-    sems,
 ):
     heads, tokens = rates_ref.shape
-    size = inputs_ref.shape[3]
-    rate_copy = pltpu.make_async_copy(rate_hbm, rates_ref, sems.at[0])
-    rate_copy.start()
-    copies = []
-    for h in range(heads):
-        for n, source in enumerate((query_hbm, key_hbm, value_hbm)):
-            copy = pltpu.make_async_copy(
-                source.at[:, pl.ds(h * size, size)], inputs_ref.at[h, n], sems.at[1 + 3 * h + n]
-            )
-            copy.start()
-            copies.append(copy)
+    size = query_ref.shape[1] // heads
     for h in range(heads):
         gain_out_ref[h : h + 1] = gain_ref[pl.ds(head_group_ref[0] * heads + h, 1), :]
-    rate_copy.wait()
     upto, _ = chunk_sums(rates_ref[...], after=False)
     count = len(upto)
     stacked = -jnp.concatenate(upto, axis=0) * LOG2_E
@@ -132,18 +121,16 @@
     place_t = lax.broadcasted_iota(jnp.int32, (span, span), 0)
     place_s = lax.broadcasted_iota(jnp.int32, (span, span), 1)
     for h in range(heads):
-        for copy in copies[3 * h : 3 * h + 3]:
-            copy.wait()
         at_h = slice(h * size, (h + 1) * size)
         places = [n * heads + h for n in range(count)]
         column = jnp.concatenate([columns[:, n : n + 1] for n in places], axis=0) - 0.5 * math.log2(size)
         row = jnp.concatenate([stacked[n : n + 1] for n in places], axis=1)
-        parts_ref[0, :, at_h] = (inputs_ref[h, 0].astype(F32) * jnp.exp2(column)).astype(BF16)
+        parts_ref[0, :, at_h] = (query_ref[:, at_h].astype(F32) * jnp.exp2(column)).astype(BF16)
         for first in range(0, tokens, span):
             at_s = slice(first, first + span)
             scores = lax.dot_general(
-                inputs_ref[h, 0, first:, :],
-                inputs_ref[h, 1, at_s, :],
+                query_ref[first:, at_h],
+                key_ref[at_s, at_h],
                 (((1,), (1,)), ((), ())),
                 preferred_element_type=F32,
             )
@@ -153,7 +140,7 @@
                 if start == first:
                     spread = jnp.where(place_t >= place_s, spread, -jnp.inf)
                 weights.append((scores[start - first : start - first + span] * jnp.exp2(spread)).astype(BF16))
-            part = jnp.dot(jnp.concatenate(weights, axis=0), inputs_ref[h, 2, at_s, :], preferred_element_type=F32)
+            part = jnp.dot(jnp.concatenate(weights, axis=0), value_ref[at_s, at_h], preferred_element_type=F32)
             if first == 0:
                 total_ref[...] = part
             else:
@@ -161,7 +148,7 @@
         parts_ref[1, :, at_h] = total_ref[...].astype(BF16)
 
 
-def finish_kernel(span, parts_ref, incoming_ref, gain_ref, out_ref):
+def finish_kernel(span, first_row, parts_ref, incoming_ref, gain_ref, out_ref):
     tokens = parts_ref.shape[1]
     heads, size, _ = incoming_ref.shape
     mean_of = jnp.full((size, size), 1.0 / size, BF16)
@@ -175,7 +162,24 @@
             center = jnp.dot(retained, mean_of, preferred_element_type=F32)
             deviation = retained.astype(F32) - center
             variance = jnp.sum(deviation * deviation, axis=1, keepdims=True) * (1.0 / size)
-            out_ref[at, columns] = (deviation * lax.rsqrt(variance + 1e-05) * gain).astype(BF16)
+            to = (first - first_row) % tokens
+            out_ref[to : to + span, columns] = (deviation * lax.rsqrt(variance + 1e-05) * gain).astype(BF16)
+
+
+def lay_out_kernel(first, in_ref, out_hbm, sems):
+    owners, _, features = in_ref.shape
+    copies = []
+    for n in range(owners):
+        columns = pl.ds((n + first) % owners * features, features)
+        copies.append(pltpu.make_async_copy(in_ref.at[n], out_hbm.at[:, columns], sems.at[n]))
+    for copy in copies:
+        copy.start()
+    for copy in copies:
+        copy.wait()
+
+
+def exchange(slots, axis, order):
+    return lax.all_to_all(slots, axis, 0, 0, tiled=True, axis_index_groups=[order])
 
 
 def per_device(queries, keys, values, decay_rate, gain):
@@ -206,23 +210,19 @@
             ],
             cost_estimate=pl.CostEstimate(flops=2 * heads * tokens * size * size, bytes_accessed=4 * tokens * features, transcendentals=0),
         )(rates, keys, values)
+    seq_order = [(n + FIRST_SEQ) % blocks for n in range(blocks)]
     slots = payload.reshape(blocks, SLOT // 2, 2, size)
-    gathered = lax.all_to_all(slots, "seq", 0, 0, tiled=True).reshape(blocks * SLOT, size)
+    gathered = exchange(slots, "seq", seq_order).reshape(blocks * SLOT, size)
     with jax.named_scope("within"):
         parts, my_gain = pl.pallas_call(
             functools.partial(within_kernel, 256),
-            in_specs=[in_smem, in_vmem] + [in_hbm] * 4,
+            in_specs=[in_smem] + [in_vmem] * 5,
             out_specs=[in_vmem] * 2,
             out_shape=[
                 jax.ShapeDtypeStruct((2, tokens, features), BF16),
                 jax.ShapeDtypeStruct((heads, size), F32),
             ],
-            scratch_shapes=[
-                pltpu.VMEM((heads, tokens), F32),
-                pltpu.VMEM((heads, 3, tokens, size), BF16),
-                pltpu.VMEM((tokens, size), F32),
-                pltpu.SemaphoreType.DMA((1 + 3 * heads,)),
-            ],
+            scratch_shapes=[pltpu.VMEM((tokens, size), F32)],
             compiler_params=pltpu.CompilerParams(vmem_limit_bytes=LARGE_VMEM),
             cost_estimate=pl.CostEstimate(
                 flops=3 * heads * tokens * tokens * size, bytes_accessed=12 * tokens * features, transcendentals=heads * tokens * tokens
@@ -231,24 +231,32 @@
     gathered, parts, my_gain = lax.optimization_barrier((gathered, parts, my_gain))
     with jax.named_scope("block_scan"):
         before = pl.pallas_call(
-            scan_kernel,
+            functools.partial(scan_kernel, seq_order),
             in_specs=[in_vmem],
             out_specs=in_vmem,
             out_shape=jax.ShapeDtypeStruct((blocks, 8, size), BF16),
             compiler_params=params,
         )(gathered)
-    incoming = lax.all_to_all(before, "seq", 0, 0, tiled=True).reshape(heads, size, size)
+    incoming = exchange(before, "seq", seq_order).reshape(heads, size, size)
     with jax.named_scope("finish"):
         normed = pl.pallas_call(
-            functools.partial(finish_kernel, 256),
+            functools.partial(finish_kernel, 256, FIRST_HEAD * (tokens // owners)),
             in_specs=[in_vmem] * 3,
             out_specs=in_vmem,
             out_shape=jax.ShapeDtypeStruct((tokens, features), BF16),
             compiler_params=params,
         )(parts, incoming, my_gain)
     sent = normed.reshape(owners, tokens // owners, features)
-    got = lax.all_to_all(sent, "head", 0, 0, tiled=True)
-    return got.transpose(1, 0, 2).reshape(tokens // owners, owners * features)
+    got = exchange(sent, "head", [(n + FIRST_HEAD) % owners for n in range(owners)])
+    with jax.named_scope("lay_out"):
+        return pl.pallas_call(
+            functools.partial(lay_out_kernel, FIRST_HEAD),
+            in_specs=[in_vmem],
+            out_specs=in_hbm,
+            out_shape=jax.ShapeDtypeStruct((tokens // owners, owners * features), BF16),
+            scratch_shapes=[pltpu.SemaphoreType.DMA((owners,))],
+            compiler_params=params,
+        )(got)
 
 
 def solution(mesh):

time: 83.8 us -> 76.1 us (0.908)
  waiting for transfers between devices: 7.56 us -> 2.42 us
  blocking collectives: 43.8 us -> 39.9 us
  starting transfers between devices: 19.3 us -> 22.2 us
  local copies, waits for them, and re-layouts: 3.54 us -> 2.46 us
    all_to_all x1, waiting for transfers between devices: 7.56 us -> 2.42 us  [exchange(): lax.all_to_all(slots, axis, 0, 0, tiled=True, axis_index_groups=[order])]
    all_to_all x2, blocking collectives: 43.8 us -> 39.9 us  [exchange(): lax.all_to_all(slots, axis, 0, 0, tiled=True, axis_index_groups=[order])]
    all_to_all x1, starting transfers between devices: 19.3 us -> 22.2 us  [exchange(): lax.all_to_all(slots, axis, 0, 0, tiled=True, axis_index_groups=[order])]
    reshape x1 -> x0, local copies, waits for them, and re-layouts: 1.08 us -> none  [per_device(): return got.transpose(1, 0, 2).reshape(tokens // owners, owners * features)]
    pallas_call x3 -> x4, Pallas kernels: 6.24 us -> 5.82 us  [the longest x1 3.59 us: per_device(): pl.pallas_call(functools.partial(within_kernel, 256), in_specs=[in_smem]...]
  transfers between devices with their start and end apart: 1 -> 1, of which waited for: 1 -> 1; matrix products, arithmetic and copies ran while one was open for 0% -> 0% of each run, Pallas kernels for 6% -> 5%
where the time goes in v3:
time: 76.1 us; the launch traced here: 75.8 us
  blocking collectives  39.9 us (52%)
  starting transfers between devices  22.2 us (29%)
  Pallas kernels  8.78 us (12%)
  local copies, waits for them, and re-layouts  2.46 us (3%)
  waiting for transfers between devices  2.42 us (3%)
    all_to_all x2, blocking collectives, exchange(): lax.all_to_all(slots, axis, 0, 0, tiled=True, axis_index_groups=[order])  39.9 us
    all_to_all x1, starting transfers between devices, exchange(): lax.all_to_all(slots, axis, 0, 0, tiled=True, axis_index_groups=[order])  22.2 us
    pallas_call x1, Pallas kernels, per_device(): pl.pallas_call(functools.partial(within_kernel, 256), in_specs=[in_smem]...  3.59 us
    pallas_call x1, Pallas kernels, per_device(): pl.pallas_call(summary_kernel, in_specs=[in_hbm] * 3, out_specs=in_vmem,...  2.96 us
    unnamed x10, local copies, waits for them, and re-layouts  2.46 us
    all_to_all x1, waiting for transfers between devices, exchange(): lax.all_to_all(slots, axis, 0, 0, tiled=True, axis_index_groups=[order])  2.42 us
  transfers between devices with their start and end apart: 1, of which 1 were waited for; matrix products, arithmetic and copies ran while one was open for 0% of the time, Pallas kernels for 5%

profile of v3, /device:TPU:1, one launch (start us, length us, event | category | flops | bytes accessed | tf_op | source)
XLA Modules:
  0.0 75.8 jit_solution(17199768027717055174)
XLA Ops:
  0.0 0.0 copy-start
  0.0 0.0 copy-start.2
  0.0 0.0 copy-start.4
  0.0 3.0 %summaries.1 = bf16[640,128]{1,0:T(8,128)(2,1)} custom-call(f32[4,1024]{1,0:T(4,128)} %bitcast.10, bf16[1024,512]{1,0:T(8,128)(2,1)} %key_ref.1, bf16[1024,512]{1,0:T(8,128)(2,1)} %value_ref.1), custom_call_target="tpu_custom_call" | custom-call | flops 134217728 | bytes 2097152 | tf_op jit(solution)/shard_map/summaries/pallas_call | solution.py:200
  3.0 22.2 %all-to-all-start = ((bf16[64,5,2,128]{3,2,1,0:T(2,128)(2,1)}), bf16[64,5,2,128]{3,2,1,0:T(2,128)(2,1)S(1)}, u32[]{:S(2)}, u32[]{:S(2)}) async-start(bf16[64,5,2,128]{3,2,1,0:T(2,128)(2,1)} %bitcast.13), calls=%async_computation | async-start | bytes 327680 | tf_op jit(solution)/shard_map/all_to_all | solution.py:182
  25.1 0.0 copy-done
  25.2 0.0 copy-done.2
  25.2 0.0 copy-done.4
  25.2 0.0 copy-start.1
  25.2 1.2 %copy-done.1 = bf16[1024,512]{1,0:T(8,128)(2,1)S(1)} copy-done((bf16[1024,512]{1,0:T(8,128)(2,1)S(1)}, bf16[1024,512]{1,0:T(8,128)(2,1)}, u32[]{:S(2)}) %copy-start.1) | copy-done | bytes 1048600
  26.4 0.0 copy-start.3
  26.4 1.2 %copy-done.3 = bf16[1024,512]{1,0:T(8,128)(2,1)S(1)} copy-done((bf16[1024,512]{1,0:T(8,128)(2,1)S(1)}, bf16[1024,512]{1,0:T(8,128)(2,1)}, u32[]{:S(2)}) %copy-start.3) | copy-done | bytes 1048600
  27.6 3.6 %within.1 = (bf16[2,1024,512]{2,1,0:T(8,128)(2,1)S(1)}, f32[4,128]{1,0:T(4,128)S(1)}) custom-call(s32[1]{0:T(128)} %bitcast.3.head_group_ref, f32[32,128]{1,0:T(8,128)S(1)} %bitcast.12, f32[4,1024]{1,0:T(4,128)S(1)} %bitcast.11, bf16[1024,512]{1,0:T(8,128)(2,1)S(1)} %copy-done.3, bf16[1024,512]{1,0:T(8,128)(2,1)S(1)} %copy-done, bf16[1024,512]{1,0:T(8,128)(2,1)S(1)} %copy-done.1), custom_call_target="tpu_custom_call" | custom-call | flops 1610612736 | bytes 6291456 | tf_op jit(solution)/shard_map/within/pallas_call | solution.py:217
  31.2 2.4 %all-to-all-done = bf16[64,5,2,128]{3,2,1,0:T(2,128)(2,1)S(1)} async-done(((bf16[64,5,2,128]{3,2,1,0:T(2,128)(2,1)}), bf16[64,5,2,128]{3,2,1,0:T(2,128)(2,1)S(1)}, u32[]{:S(2)}, u32[]{:S(2)}) %all-to-all-start) | async-done | bytes 163872 | tf_op jit(solution)/shard_map/all_to_all | solution.py:182
  33.7 0.1 block_scan.1
  33.8 20.5 %all_to_all.15 = bf16[64,8,128]{2,1,0:T(8,128)(2,1)S(1)} all-to-all(bf16[64,8,128]{2,1,0:T(8,128)(2,1)S(1)} %block_scan.1), channel_id=1, replica_groups={{328,336,344,352,360,368,376,384,392,400,408,416,424,432,440,448,456,46..., dimensions={0} | all-to-all | bytes 262144 | tf_op jit(solution)/shard_map/all_to_all | solution.py:182
  54.3 1.1 %finish.1 = bf16[1024,512]{1,0:T(8,128)(2,1)S(1)} custom-call(bf16[2,1024,512]{2,1,0:T(8,128)(2,1)S(1)} %get-tuple-element.12.parts_ref, bf16[4,128,128]{2,1,0:T(8,128)(2,1)S(1)} %bitcast.9, f32[4,128]{1,0:T(4,128)S(1)} %get-tuple-element.14.gain_ref), custom_call_target="tpu_custom_call" | custom-call | tf_op jit(solution)/shard_map/finish/pallas_call | solution.py:242
  55.4 19.4 %all_to_all.16.in_ref = bf16[8,128,512]{2,1,0:T(8,128)(2,1)S(1)} all-to-all(bf16[8,128,512]{2,1,0:T(8,128)(2,1)S(1)} %bitcast.7), channel_id=1, replica_groups={{4,5,6,7,0,1,2,3},{12,13,14,15,8,9,10,11},{20,21,22,23,16,17,18,19},{28..., dimensions={0} | all-to-all | bytes 2097152 | tf_op jit(solution)/shard_map/all_to_all | solution.py:182
  74.8 1.0 %lay_out.1 = bf16[128,4096]{1,0:T(8,128)(2,1)} custom-call(bf16[8,128,512]{2,1,0:T(8,128)(2,1)S(1)} %all_to_all.16.in_ref), custom_call_target="tpu_custom_call" | custom-call | tf_op jit(solution)/shard_map/lay_out/pallas_call | solution.py:252
Async XLA Ops:
  0.0 25.2 %copy-start = (bf16[1024,512]{1,0:T(8,128)(2,1)S(1)}, bf16[1024,512]{1,0:T(8,128)(2,1)}, u32[]{:S(2)}) copy-start(bf16[1024,512]{1,0:T(8,128)(2,1)} %key_ref.1) | copy-start | bytes 3145732
  0.0 25.2 %copy-start.2 = (f32[1024,4]{0,1:T(4,128)S(1)}, f32[1024,4]{0,1:T(4,128)}, u32[]{:S(2)}) copy-start(f32[1024,4]{0,1:T(4,128)} %param.8) | copy-start | bytes 49156
  0.0 25.2 %copy-start.4 = (f32[4096]{0:T(1024)S(1)}, f32[4096]{0:T(1024)}, u32[]{:S(2)}) copy-start(f32[4096]{0:T(1024)} %param.9) | copy-start | bytes 49156
  3.0 30.7 %all-to-all-start = ((bf16[64,5,2,128]{3,2,1,0:T(2,128)(2,1)}), bf16[64,5,2,128]{3,2,1,0:T(2,128)(2,1)S(1)}, u32[]{:S(2)}, u32[]{:S(2)}) async-start(bf16[64,5,2,128]{3,2,1,0:T(2,128)(2,1)} %bitcast.13), calls=%async_computation | async-start | bytes 327680 | tf_op jit(solution)/shard_map/all_to_all | solution.py:182
  25.2 1.2 %copy-start.1 = (bf16[1024,512]{1,0:T(8,128)(2,1)S(1)}, bf16[1024,512]{1,0:T(8,128)(2,1)}, u32[]{:S(2)}) copy-start(bf16[1024,512]{1,0:T(8,128)(2,1)} %value_ref.1) | copy-start | bytes 3145732
  26.4 1.2 %copy-start.3 = (bf16[1024,512]{1,0:T(8,128)(2,1)S(1)}, bf16[1024,512]{1,0:T(8,128)(2,1)}, u32[]{:S(2)}) copy-start(bf16[1024,512]{1,0:T(8,128)(2,1)} %query_ref.1) | copy-start | bytes 3145732

commit v4 on v3

--- a/solution.py
+++ b/solution.py
@@ -11,8 +11,11 @@
 LANE = 128
 F32 = jnp.float32
 BF16 = jnp.bfloat16
-SLOT = 10
-FIRST_SEQ = 41
+PARTS = 8
+QUAD = 4
+NEAR = [1, 2, 3, 0]
+FAR = [2, 3, 1, 0]
+ROWS = [2, 3, 1, 0]
 FIRST_HEAD = 4
 LOG2_E = 1.4426950408889634
 SMALL_VMEM = 16 * 1024 * 1024
@@ -49,6 +52,18 @@
     return pieces, running
 
 
+def put_state(ref, at, state, keep):
+    parts = [p.astype(F32) for p in split_three(keep)]
+    parts.append(jnp.zeros((PARTS - len(parts), LANE), F32))
+    ref[at] = jnp.concatenate([state] + parts, axis=0).astype(BF16)
+
+
+def take_state(ref, at):
+    rows = ref[at].astype(F32)
+    size = rows.shape[0] - PARTS
+    return rows[:size], rows[size : size + 1] + rows[size + 1 : size + 2] + rows[size + 2 : size + 3]
+
+
 def summary_kernel(rate_hbm, key_hbm, value_hbm, out_ref, rates_ref, key_ref, value_ref, sems):
     heads, tokens = rates_ref.shape
     size = key_ref.shape[1] // heads
@@ -76,31 +91,46 @@
         codes = (summary / scales).astype(BF16)
         restored = codes.astype(F32) * scales
         keep = jnp.broadcast_to(keeps[h : h + 1], (1, LANE))
-        parts = [p.astype(F32) for p in split_three(keep)[:2]]
-        chunks = size // 8
-        for start in range(0, chunks, 8):
-            rows = []
-            for i in range(start, start + 8):
-                rows += [restored[i * 8 : (i + 1) * 8]] + parts
-            slot = h * chunks + start
-            out_ref[slot * SLOT : (slot + 8) * SLOT, :] = jnp.concatenate(rows, axis=0).astype(BF16)
-
-
-def scan_kernel(order, in_ref, out_ref):
-    state = jnp.zeros((8, LANE), F32)
-    groups = [in_ref[n * SLOT : (n + 8) * SLOT, :].astype(F32) for n in range(0, len(order), 8)]
-    for block in range(len(order)):
-        slot = order.index(block)
-        out_ref[slot] = state.astype(BF16)
-        rows = groups[slot // 8]
-        at = slot % 8 * SLOT
-        keep = rows[at + 8 : at + 9] + rows[at + 9 : at + 10]
-        state = state * keep + rows[at : at + 8]
+        slots = out_ref.shape[0] // heads
+        part = size // slots
+        for n in range(slots):
+            put_state(out_ref, (h * slots + n,), restored[n * part : (n + 1) * part], keep)
+
+
+def slot_of(row, near):
+    return ROWS.index(row) * QUAD + NEAR.index(near)
+
+
+def total_kernel(in_ref, out_ref):
+    for row in range(QUAD):
+        state, keep = take_state(in_ref, (slot_of(row, 0),))
+        for near in range(1, QUAD):
+            more, more_keep = take_state(in_ref, (slot_of(row, near),))
+            state = state * more_keep + more
+            keep = keep * more_keep
+        for n in range(QUAD):
+            put_state(out_ref, (n, row), state, keep)
+
+
+def carry_kernel(place_ref, groups_ref, blocks_ref, out_ref):
+    mine = place_ref[0] // QUAD % QUAD
+    carry = jnp.zeros(out_ref.shape[1:], F32)
+    for row in range(QUAD):
+        start = carry
+        for far in range(QUAD):
+            start = jnp.where(mine == far, carry, start)
+            state, keep = take_state(groups_ref, (FAR.index(far), row))
+            carry = carry * keep + state
+        for near in range(QUAD):
+            slot = slot_of(row, near)
+            out_ref[slot] = start.astype(BF16)
+            state, keep = take_state(blocks_ref, (slot,))
+            start = start * keep + state
 
 
 def within_kernel(
     span,
-    head_group_ref,
+    place_ref,
     gain_ref,
     rates_ref,
     query_ref,
@@ -108,12 +138,14 @@
     value_ref,
     parts_ref,
     gain_out_ref,
+    place_out_ref,
     total_ref,
 ):
     heads, tokens = rates_ref.shape
     size = query_ref.shape[1] // heads
-    for h in range(heads):
-        gain_out_ref[h : h + 1] = gain_ref[pl.ds(head_group_ref[0] * heads + h, 1), :]
+    place_out_ref[0] = place_ref[1]
+    for h in range(heads):
+        gain_out_ref[h : h + 1] = gain_ref[pl.ds(place_ref[0] * heads + h, 1), :]
     upto, _ = chunk_sums(rates_ref[...], after=False)
     count = len(upto)
     stacked = -jnp.concatenate(upto, axis=0) * LOG2_E
@@ -178,8 +210,16 @@
         copy.wait()
 
 
-def exchange(slots, axis, order):
-    return lax.all_to_all(slots, axis, 0, 0, tiled=True, axis_index_groups=[order])
+def near_groups():
+    return [
+        [(row * QUAD + far) * QUAD + near for row in ROWS for near in NEAR] for far in range(QUAD)
+    ]
+
+
+def far_groups():
+    return [
+        [(row * QUAD + far) * QUAD + near for far in FAR] for row in range(QUAD) for near in range(QUAD)
+    ]
 
 
 def per_device(queries, keys, values, decay_rate, gain):
@@ -194,14 +234,20 @@
     in_hbm = pl.BlockSpec(memory_space=pl.ANY)
     in_vmem = pl.BlockSpec(memory_space=pltpu.VMEM)
     in_smem = pl.BlockSpec(memory_space=pltpu.SMEM)
-    head_group = lax.axis_index("head").astype(jnp.int32).reshape(1)
+    place = jnp.stack([lax.axis_index("head"), lax.axis_index("seq")]).astype(jnp.int32)
+    part = heads * size // QUAD**2
+    block_shape = jax.ShapeDtypeStruct((QUAD**2, part + PARTS, size), BF16)
+    group_shape = jax.ShapeDtypeStruct((QUAD, QUAD, part + PARTS, size), BF16)
+
+    def swap(sent, groups):
+        return lax.all_to_all(sent, "seq", 0, 0, tiled=True, axis_index_groups=groups)
 
     with jax.named_scope("summaries"):
         payload = pl.pallas_call(
             summary_kernel,
             in_specs=[in_hbm] * 3,
             out_specs=in_vmem,
-            out_shape=jax.ShapeDtypeStruct((blocks * SLOT, size), BF16),
+            out_shape=block_shape,
             scratch_shapes=[
                 pltpu.VMEM((heads, tokens), F32),
                 pltpu.VMEM((tokens, features), BF16),
@@ -210,34 +256,39 @@
             ],
             cost_estimate=pl.CostEstimate(flops=2 * heads * tokens * size * size, bytes_accessed=4 * tokens * features, transcendentals=0),
         )(rates, keys, values)
-    seq_order = [(n + FIRST_SEQ) % blocks for n in range(blocks)]
-    slots = payload.reshape(blocks, SLOT // 2, 2, size)
-    gathered = exchange(slots, "seq", seq_order).reshape(blocks * SLOT, size)
+    block_states = swap(payload, near_groups())
+    with jax.named_scope("group_totals"):
+        group_totals = pl.pallas_call(
+            total_kernel, in_specs=[in_vmem], out_specs=in_vmem, out_shape=group_shape, compiler_params=params
+        )(block_states)
+    group_states = swap(group_totals, far_groups())
+    block_states, late_rates = lax.optimization_barrier((block_states, rates))
     with jax.named_scope("within"):
-        parts, my_gain = pl.pallas_call(
+        parts, my_gain, my_place = pl.pallas_call(
             functools.partial(within_kernel, 256),
             in_specs=[in_smem] + [in_vmem] * 5,
-            out_specs=[in_vmem] * 2,
+            out_specs=[in_vmem] * 2 + [in_smem],
             out_shape=[
                 jax.ShapeDtypeStruct((2, tokens, features), BF16),
                 jax.ShapeDtypeStruct((heads, size), F32),
+                jax.ShapeDtypeStruct((1,), jnp.int32),
             ],
             scratch_shapes=[pltpu.VMEM((tokens, size), F32)],
             compiler_params=pltpu.CompilerParams(vmem_limit_bytes=LARGE_VMEM),
             cost_estimate=pl.CostEstimate(
                 flops=3 * heads * tokens * tokens * size, bytes_accessed=12 * tokens * features, transcendentals=heads * tokens * tokens
             ),
-        )(head_group, gain.reshape(-1, size), rates, queries, keys, values)
-    gathered, parts, my_gain = lax.optimization_barrier((gathered, parts, my_gain))
-    with jax.named_scope("block_scan"):
+        )(place, gain.reshape(-1, size), late_rates, queries, keys, values)
+    group_states, parts, my_gain, my_place = lax.optimization_barrier((group_states, parts, my_gain, my_place))
+    with jax.named_scope("carry"):
         before = pl.pallas_call(
-            functools.partial(scan_kernel, seq_order),
-            in_specs=[in_vmem],
+            carry_kernel,
+            in_specs=[in_smem] + [in_vmem] * 2,
             out_specs=in_vmem,
-            out_shape=jax.ShapeDtypeStruct((blocks, 8, size), BF16),
+            out_shape=jax.ShapeDtypeStruct((QUAD**2, part, size), BF16),
             compiler_params=params,
-        )(gathered)
-    incoming = exchange(before, "seq", seq_order).reshape(heads, size, size)
+        )(my_place, group_states, block_states)
+    incoming = swap(before, near_groups()).reshape(heads, size, size)
     with jax.named_scope("finish"):
         normed = pl.pallas_call(
             functools.partial(finish_kernel, 256, FIRST_HEAD * (tokens // owners)),
@@ -247,7 +298,8 @@
             compiler_params=params,
         )(parts, incoming, my_gain)
     sent = normed.reshape(owners, tokens // owners, features)
-    got = exchange(sent, "head", [(n + FIRST_HEAD) % owners for n in range(owners)])
+    head_order = [(n + FIRST_HEAD) % owners for n in range(owners)]
+    got = lax.all_to_all(sent, "head", 0, 0, tiled=True, axis_index_groups=[head_order])
     with jax.named_scope("lay_out"):
         return pl.pallas_call(
             functools.partial(lay_out_kernel, FIRST_HEAD),

time: 76.1 us -> 73.8 us (0.970)
  starting transfers between devices: 22.2 us -> 14.3 us
  blocking collectives: 39.9 us -> 45.7 us
  waiting for transfers between devices: 2.42 us -> 0.01 us
  Pallas kernels: 8.78 us -> 10.8 us
    all_to_all x1, starting transfers between devices: 22.2 us -> 14.3 us  [swap(): lax.all_to_all(sent, 'seq', 0, 0, tiled=True, axis_index_groups=groups)]
    all_to_all x2 -> x3, blocking collectives: 39.9 us -> 45.7 us  [the longest x2 24.1 us: swap(): lax.all_to_all(sent, 'seq', 0, 0, tiled=True, axis_index_groups=groups)]
    all_to_all x1, waiting for transfers between devices: 2.42 us -> 0.01 us  [swap(): lax.all_to_all(sent, 'seq', 0, 0, tiled=True, axis_index_groups=groups)]
    pallas_call x1 -> x2, Pallas kernels: 0.15 us -> 1.36 us  [the longest x1 0.72 us: per_device(): pl.pallas_call(total_kernel, in_specs=[in_vmem], out_specs=in_vmem, out_s...]
    pallas_call x1, Pallas kernels: 3.59 us -> 4.38 us  [per_device(): pl.pallas_call(functools.partial(within_kernel, 256), in_specs=[in_smem]...]
  transfers between devices with their start and end apart: 1 -> 1, of which waited for: 1 -> 0; matrix products, arithmetic and copies ran while one was open for 0% -> 0% of each run, Pallas kernels for 5% -> 6%
where the time goes in v4:
time: 73.8 us; the launch traced here: 73.4 us
  blocking collectives  45.7 us (62%)
  starting transfers between devices  14.3 us (19%)
  Pallas kernels  10.8 us (15%)
  local copies, waits for them, and re-layouts  2.46 us (3%)
    all_to_all x2, blocking collectives, swap(): lax.all_to_all(sent, 'seq', 0, 0, tiled=True, axis_index_groups=groups)  24.1 us
    all_to_all x1, blocking collectives, per_device(): lax.all_to_all(sent, 'head', 0, 0, tiled=True, axis_index_groups=[head_or...  21.6 us
    all_to_all x1, starting transfers between devices, swap(): lax.all_to_all(sent, 'seq', 0, 0, tiled=True, axis_index_groups=groups)  14.3 us
    pallas_call x1, Pallas kernels, per_device(): pl.pallas_call(functools.partial(within_kernel, 256), in_specs=[in_smem]...  4.38 us
    pallas_call x1, Pallas kernels, per_device(): pl.pallas_call(summary_kernel, in_specs=[in_hbm] * 3, out_specs=in_vmem,...  2.96 us
    unnamed x10, local copies, waits for them, and re-layouts  2.46 us
  transfers between devices with their start and end apart: 1, of which 0 were waited for; matrix products, arithmetic and copies ran while one was open for 0% of the time, Pallas kernels for 6%

profile of v4, /device:TPU:1, one launch (start us, length us, event | category | flops | bytes accessed | tf_op | source)
XLA Modules:
  0.0 73.4 jit_solution(16281730741075995063)
XLA Ops:
  0.0 0.0 copy-start
  0.0 0.0 copy-start.2
  0.0 0.0 copy-start.4
  0.0 3.0 %summaries.1 = bf16[16,40,128]{2,1,0:T(8,128)(2,1)} custom-call(f32[4,1024]{1,0:T(4,128)} %bitcast.8, bf16[1024,512]{1,0:T(8,128)(2,1)} %key_ref.1, bf16[1024,512]{1,0:T(8,128)(2,1)} %value_ref.1), custom_call_target="tpu_custom_call" | custom-call | flops 134217728 | bytes 2097152 | tf_op jit(solution)/shard_map/summaries/pallas_call | solution.py:246
  3.0 14.5 %all_to_all.20.in_ref.blocks_ref = bf16[16,40,128]{2,1,0:T(8,128)(2,1)S(1)} all-to-all(bf16[16,40,128]{2,1,0:T(8,128)(2,1)} %summaries.1), channel_id=1, replica_groups={{264,272,280,256,392,400,408,384,136,144,152,128,8,16,24,0},{296,304,31..., dimensions={0} | all-to-all | bytes 327680 | tf_op jit(solution)/shard_map/all_to_all | solution.py:243
  17.5 0.7 group_totals.1
  18.2 14.3 %all-to-all-start.1 = ((bf16[4,4,40,128]{3,2,1,0:T(8,128)(2,1)}), bf16[4,4,40,128]{3,2,1,0:T(8,128)(2,1)S(1)}, u32[]{:S(2)}, u32[]{:S(2)}) async-start(bf16[4,4,40,128]{3,2,1,0:T(8,128)(2,1)} %group_totals.1), calls=%async_computation.1 | async-start | bytes 327680 | tf_op jit(solution)/shard_map/all_to_all | solution.py:243
  32.5 0.1 pad_add_fusion.place_ref
  32.6 0.0 copy-done
  32.6 0.0 copy-done.2
  32.6 0.0 copy-done.4
  32.6 0.0 copy-start.1
  32.6 1.2 %copy-done.1 = bf16[1024,512]{1,0:T(8,128)(2,1)S(1)} copy-done((bf16[1024,512]{1,0:T(8,128)(2,1)S(1)}, bf16[1024,512]{1,0:T(8,128)(2,1)}, u32[]{:S(2)}) %copy-start.1) | copy-done | bytes 1048600
  33.8 0.0 copy-start.3
  33.8 1.2 %copy-done.3 = bf16[1024,512]{1,0:T(8,128)(2,1)S(1)} copy-done((bf16[1024,512]{1,0:T(8,128)(2,1)S(1)}, bf16[1024,512]{1,0:T(8,128)(2,1)}, u32[]{:S(2)}) %copy-start.3) | copy-done | bytes 1048600
  35.1 4.4 %within.1 = (bf16[2,1024,512]{2,1,0:T(8,128)(2,1)S(1)}, f32[4,128]{1,0:T(4,128)S(1)}, s32[1]{0:T(128)}) custom-call(s32[2]{0:T(128)S(1)} %pad_add_fusion.place_ref, f32[32,128]{1,0:T(8,128)S(1)} %bitcast.10, f32[4,1024]{1,0:T(4,128)S(1)} %bitcast.9, bf16[1024,512]{1,0:T(8,128)(2,1)S(1)} %copy-done.3, bf16[1024,512]{1,0:T(8,128)(2,1)S(1)} %copy-done, ...), custom_call_target="tpu_custom_call" | custom-call | flops 1610612736 | bytes 6291456 | tf_op jit(solution)/shard_map/within/pallas_call | solution.py:267
  39.5 0.0 all-to-all-done.1.groups_ref
  39.5 0.6 carry.1
  40.1 9.6 %all_to_all.21 = bf16[16,32,128]{2,1,0:T(8,128)(2,1)S(1)} all-to-all(bf16[16,32,128]{2,1,0:T(8,128)(2,1)S(1)} %carry.1), channel_id=1, replica_groups={{264,272,280,256,392,400,408,384,136,144,152,128,8,16,24,0},{296,304,31..., dimensions={0} | all-to-all | bytes 262144 | tf_op jit(solution)/shard_map/all_to_all | solution.py:243
  49.7 1.1 %finish.1 = bf16[1024,512]{1,0:T(8,128)(2,1)S(1)} custom-call(bf16[2,1024,512]{2,1,0:T(8,128)(2,1)S(1)} %get-tuple-element.18.parts_ref, bf16[4,128,128]{2,1,0:T(8,128)(2,1)S(1)} %bitcast.7, f32[4,128]{1,0:T(4,128)S(1)} %get-tuple-element.22.gain_ref), custom_call_target="tpu_custom_call" | custom-call | tf_op jit(solution)/shard_map/finish/pallas_call | solution.py:293
  50.8 21.6 %all_to_all.22.in_ref = bf16[8,128,512]{2,1,0:T(8,128)(2,1)S(1)} all-to-all(bf16[8,128,512]{2,1,0:T(8,128)(2,1)S(1)} %bitcast.6), channel_id=1, replica_groups={{4,5,6,7,0,1,2,3},{12,13,14,15,8,9,10,11},{20,21,22,23,16,17,18,19},{28..., dimensions={0} | all-to-all | bytes 2097152 | tf_op jit(solution)/shard_map/all_to_all | solution.py:302
  72.3 1.0 %lay_out.1 = bf16[128,4096]{1,0:T(8,128)(2,1)} custom-call(bf16[8,128,512]{2,1,0:T(8,128)(2,1)S(1)} %all_to_all.22.in_ref), custom_call_target="tpu_custom_call" | custom-call | tf_op jit(solution)/shard_map/lay_out/pallas_call | solution.py:304
Async XLA Ops:
  0.0 32.6 %copy-start = (bf16[1024,512]{1,0:T(8,128)(2,1)S(1)}, bf16[1024,512]{1,0:T(8,128)(2,1)}, u32[]{:S(2)}) copy-start(bf16[1024,512]{1,0:T(8,128)(2,1)} %key_ref.1) | copy-start | bytes 3145732
  0.0 32.6 %copy-start.2 = (f32[1024,4]{0,1:T(4,128)S(1)}, f32[1024,4]{0,1:T(4,128)}, u32[]{:S(2)}) copy-start(f32[1024,4]{0,1:T(4,128)} %param.8) | copy-start | bytes 49156
  0.0 32.6 %copy-start.4 = (f32[4096]{0:T(1024)S(1)}, f32[4096]{0:T(1024)}, u32[]{:S(2)}) copy-start(f32[4096]{0:T(1024)} %param.9) | copy-start | bytes 49156
  18.2 21.2 %all-to-all-start.1 = ((bf16[4,4,40,128]{3,2,1,0:T(8,128)(2,1)}), bf16[4,4,40,128]{3,2,1,0:T(8,128)(2,1)S(1)}, u32[]{:S(2)}, u32[]{:S(2)}) async-start(bf16[4,4,40,128]{3,2,1,0:T(8,128)(2,1)} %group_totals.1), calls=%async_computation.1 | async-start | bytes 327680 | tf_op jit(solution)/shard_map/all_to_all | solution.py:243
  32.6 1.2 %copy-start.1 = (bf16[1024,512]{1,0:T(8,128)(2,1)S(1)}, bf16[1024,512]{1,0:T(8,128)(2,1)}, u32[]{:S(2)}) copy-start(bf16[1024,512]{1,0:T(8,128)(2,1)} %value_ref.1) | copy-start | bytes 3145732
  33.8 1.2 %copy-start.3 = (bf16[1024,512]{1,0:T(8,128)(2,1)S(1)}, bf16[1024,512]{1,0:T(8,128)(2,1)}, u32[]{:S(2)}) copy-start(bf16[1024,512]{1,0:T(8,128)(2,1)} %query_ref.1) | copy-start | bytes 3145732

commit v5 on v4

--- a/solution.py
+++ b/solution.py
@@ -11,7 +11,7 @@
 LANE = 128
 F32 = jnp.float32
 BF16 = jnp.bfloat16
-PARTS = 8
+PARTS = 2
 QUAD = 4
 NEAR = [1, 2, 3, 0]
 FAR = [2, 3, 1, 0]
@@ -52,16 +52,23 @@
     return pieces, running
 
 
-def put_state(ref, at, state, keep):
-    parts = [p.astype(F32) for p in split_three(keep)]
-    parts.append(jnp.zeros((PARTS - len(parts), LANE), F32))
-    ref[at] = jnp.concatenate([state] + parts, axis=0).astype(BF16)
-
-
-def take_state(ref, at):
-    rows = ref[at].astype(F32)
-    size = rows.shape[0] - PARTS
-    return rows[:size], rows[size : size + 1] + rows[size + 1 : size + 2] + rows[size + 2 : size + 3]
+def pack_states(states):
+    rows = []
+    for state, keep in states:
+        rows += [state] + [p.astype(F32) for p in split_three(keep)[:PARTS]]
+    return jnp.concatenate(rows, axis=0).astype(BF16)
+
+
+def unpack_states(ref):
+    half = ref.shape[0] // 2
+    slot = ref.shape[0] // QUAD**2
+    states = []
+    for first in (0, half):
+        rows = ref[first : first + half, :].astype(F32)
+        for at in range(0, half, slot):
+            keep = rows[at + slot - 2 : at + slot - 1] + rows[at + slot - 1 : at + slot]
+            states.append((rows[at : at + slot - PARTS], keep))
+    return states
 
 
 def summary_kernel(rate_hbm, key_hbm, value_hbm, out_ref, rates_ref, key_ref, value_ref, sems):
@@ -85,16 +92,18 @@
         key_t = key_ref[:, h * size : (h + 1) * size].T
         decayed_keys.append((key_t.astype(F32) * decays[h : h + 1]).astype(BF16))
     copies[2].wait()
+    states = []
     for h in range(heads):
         summary = jnp.dot(decayed_keys[h], value_ref[:, h * size : (h + 1) * size], preferred_element_type=F32)
         scales = (jnp.max(jnp.abs(summary), axis=1, keepdims=True) + 1e-06).astype(BF16).astype(F32)
         codes = (summary / scales).astype(BF16)
         restored = codes.astype(F32) * scales
         keep = jnp.broadcast_to(keeps[h : h + 1], (1, LANE))
-        slots = out_ref.shape[0] // heads
-        part = size // slots
-        for n in range(slots):
-            put_state(out_ref, (h * slots + n,), restored[n * part : (n + 1) * part], keep)
+        part = heads * size // QUAD**2
+        states += [(restored[n : n + part], keep) for n in range(0, size, part)]
+    half = out_ref.shape[0] // 2
+    for n in range(2):
+        out_ref[n * half : (n + 1) * half, :] = pack_states(states[n * len(states) // 2 : (n + 1) * len(states) // 2])
 
 
 def slot_of(row, near):
@@ -102,29 +111,35 @@
 
 
 def total_kernel(in_ref, out_ref):
+    blocks = unpack_states(in_ref)
+    totals = []
     for row in range(QUAD):
-        state, keep = take_state(in_ref, (slot_of(row, 0),))
+        state, keep = blocks[slot_of(row, 0)]
         for near in range(1, QUAD):
-            more, more_keep = take_state(in_ref, (slot_of(row, near),))
+            more, more_keep = blocks[slot_of(row, near)]
             state = state * more_keep + more
             keep = keep * more_keep
-        for n in range(QUAD):
-            put_state(out_ref, (n, row), state, keep)
+        totals.append((state, keep))
+    packed = pack_states(totals + totals)
+    half = out_ref.shape[0] // 2
+    for n in range(2):
+        out_ref[n * half : (n + 1) * half, :] = packed
 
 
 def carry_kernel(place_ref, groups_ref, blocks_ref, out_ref):
+    groups, blocks = unpack_states(groups_ref), unpack_states(blocks_ref)
     mine = place_ref[0] // QUAD % QUAD
     carry = jnp.zeros(out_ref.shape[1:], F32)
     for row in range(QUAD):
         start = carry
         for far in range(QUAD):
             start = jnp.where(mine == far, carry, start)
-            state, keep = take_state(groups_ref, (FAR.index(far), row))
+            state, keep = groups[FAR.index(far) * QUAD + row]
             carry = carry * keep + state
         for near in range(QUAD):
             slot = slot_of(row, near)
             out_ref[slot] = start.astype(BF16)
-            state, keep = take_state(blocks_ref, (slot,))
+            state, keep = blocks[slot]
             start = start * keep + state
 
 
@@ -236,18 +251,20 @@
     in_smem = pl.BlockSpec(memory_space=pltpu.SMEM)
     place = jnp.stack([lax.axis_index("head"), lax.axis_index("seq")]).astype(jnp.int32)
     part = heads * size // QUAD**2
-    block_shape = jax.ShapeDtypeStruct((QUAD**2, part + PARTS, size), BF16)
-    group_shape = jax.ShapeDtypeStruct((QUAD, QUAD, part + PARTS, size), BF16)
+    state_shape = jax.ShapeDtypeStruct((QUAD**2 * (part + PARTS), size), BF16)
 
     def swap(sent, groups):
         return lax.all_to_all(sent, "seq", 0, 0, tiled=True, axis_index_groups=groups)
+
+    def swap_states(states, groups):
+        return swap(states.reshape(len(groups[0]), -1, 2, size), groups).reshape(states.shape)
 
     with jax.named_scope("summaries"):
         payload = pl.pallas_call(
             summary_kernel,
             in_specs=[in_hbm] * 3,
             out_specs=in_vmem,
-            out_shape=block_shape,
+            out_shape=state_shape,
             scratch_shapes=[
                 pltpu.VMEM((heads, tokens), F32),
                 pltpu.VMEM((tokens, features), BF16),
@@ -256,12 +273,12 @@
             ],
             cost_estimate=pl.CostEstimate(flops=2 * heads * tokens * size * size, bytes_accessed=4 * tokens * features, transcendentals=0),
         )(rates, keys, values)
-    block_states = swap(payload, near_groups())
+    block_states = swap_states(payload, near_groups())
     with jax.named_scope("group_totals"):
         group_totals = pl.pallas_call(
-            total_kernel, in_specs=[in_vmem], out_specs=in_vmem, out_shape=group_shape, compiler_params=params
+            total_kernel, in_specs=[in_vmem], out_specs=in_vmem, out_shape=state_shape, compiler_params=params
         )(block_states)
-    group_states = swap(group_totals, far_groups())
+    group_states = swap_states(group_totals, far_groups())
     block_states, late_rates = lax.optimization_barrier((block_states, rates))
     with jax.named_scope("within"):
         parts, my_gain, my_place = pl.pallas_call(

time: 73.8 us -> 73.6 us (level)
  no operation moved by 1% of the time
where the time goes in v5:
time: 73.6 us; the launch traced here: 73.2 us
  blocking collectives  45.5 us (62%)
  starting transfers between devices  14.3 us (19%)
  Pallas kernels  10.8 us (15%)
  local copies, waits for them, and re-layouts  2.46 us (3%)
    all_to_all x2, blocking collectives, swap(): lax.all_to_all(sent, 'seq', 0, 0, tiled=True, axis_index_groups=groups)  23.8 us
    all_to_all x1, blocking collectives, per_device(): lax.all_to_all(sent, 'head', 0, 0, tiled=True, axis_index_groups=[head_or...  21.7 us
    all_to_all x1, starting transfers between devices, swap(): lax.all_to_all(sent, 'seq', 0, 0, tiled=True, axis_index_groups=groups)  14.3 us
    pallas_call x1, Pallas kernels, per_device(): pl.pallas_call(functools.partial(within_kernel, 256), in_specs=[in_smem]...  4.38 us
    pallas_call x1, Pallas kernels, per_device(): pl.pallas_call(summary_kernel, in_specs=[in_hbm] * 3, out_specs=in_vmem,...  2.95 us
    unnamed x10, local copies, waits for them, and re-layouts  2.46 us
  transfers between devices with their start and end apart: 1, of which 0 were waited for; matrix products, arithmetic and copies ran while one was open for 0% of the time, Pallas kernels for 6%

profile of v5, /device:TPU:1, one launch (start us, length us, event | category | flops | bytes accessed | tf_op | source)
XLA Modules:
  0.0 73.2 jit_solution(7067564107245041680)
XLA Ops:
  0.0 0.0 copy-start
  0.0 0.0 copy-start.2
  0.0 0.0 copy-start.4
  0.0 3.0 %summaries.1 = bf16[544,128]{1,0:T(8,128)(2,1)} custom-call(f32[4,1024]{1,0:T(4,128)} %bitcast.15, bf16[1024,512]{1,0:T(8,128)(2,1)} %key_ref.1, bf16[1024,512]{1,0:T(8,128)(2,1)} %value_ref.1), custom_call_target="tpu_custom_call" | custom-call | flops 134217728 | bytes 2097152 | tf_op jit(solution)/shard_map/summaries/pallas_call | solution.py:263
  3.0 14.3 %all_to_all.20 = bf16[16,17,2,128]{3,2,1,0:T(2,128)(2,1)S(1)} all-to-all(bf16[16,17,2,128]{3,2,1,0:T(2,128)(2,1)} %bitcast.18), channel_id=1, replica_groups={{264,272,280,256,392,400,408,384,136,144,152,128,8,16,24,0},{296,304,31..., dimensions={0} | all-to-all | bytes 278528 | tf_op jit(solution)/shard_map/all_to_all | solution.py:257
  17.2 0.7 group_totals.1
  18.0 14.3 %all-to-all-start.1 = ((bf16[4,68,2,128]{3,2,1,0:T(2,128)(2,1)}), bf16[4,68,2,128]{3,2,1,0:T(2,128)(2,1)S(1)}, u32[]{:S(2)}, u32[]{:S(2)}) async-start(bf16[4,68,2,128]{3,2,1,0:T(2,128)(2,1)} %bitcast.3), calls=%async_computation.1 | async-start | bytes 278528 | tf_op jit(solution)/shard_map/all_to_all | solution.py:257
  32.3 0.1 pad_add_fusion.place_ref
  32.3 0.0 copy-done
  32.3 0.0 copy-done.2
  32.4 0.0 copy-done.4
  32.4 0.0 copy-start.1
  32.4 1.2 %copy-done.1 = bf16[1024,512]{1,0:T(8,128)(2,1)S(1)} copy-done((bf16[1024,512]{1,0:T(8,128)(2,1)S(1)}, bf16[1024,512]{1,0:T(8,128)(2,1)}, u32[]{:S(2)}) %copy-start.1) | copy-done | bytes 1048600
  33.6 0.0 copy-start.3
  33.6 1.2 %copy-done.3 = bf16[1024,512]{1,0:T(8,128)(2,1)S(1)} copy-done((bf16[1024,512]{1,0:T(8,128)(2,1)S(1)}, bf16[1024,512]{1,0:T(8,128)(2,1)}, u32[]{:S(2)}) %copy-start.3) | copy-done | bytes 1048600
  34.8 4.4 %within.1 = (bf16[2,1024,512]{2,1,0:T(8,128)(2,1)S(1)}, f32[4,128]{1,0:T(4,128)S(1)}, s32[1]{0:T(128)}) custom-call(s32[2]{0:T(128)S(1)} %pad_add_fusion.place_ref, f32[32,128]{1,0:T(8,128)S(1)} %bitcast.17, f32[4,1024]{1,0:T(4,128)S(1)} %bitcast.16, bf16[1024,512]{1,0:T(8,128)(2,1)S(1)} %copy-done.3, bf16[1024,512]{1,0:T(8,128)(2,1)S(1)} %copy-done, ...), custom_call_target="tpu_custom_call" | custom-call | flops 1610612736 | bytes 6291456 | tf_op jit(solution)/shard_map/within/pallas_call | solution.py:284
  39.2 0.0 all-to-all-done.1
  39.2 0.7 carry.1
  39.9 9.6 %all_to_all.21 = bf16[16,32,128]{2,1,0:T(8,128)(2,1)S(1)} all-to-all(bf16[16,32,128]{2,1,0:T(8,128)(2,1)S(1)} %carry.1), channel_id=1, replica_groups={{264,272,280,256,392,400,408,384,136,144,152,128,8,16,24,0},{296,304,31..., dimensions={0} | all-to-all | bytes 262144 | tf_op jit(solution)/shard_map/all_to_all | solution.py:257
  49.4 1.1 %finish.1 = bf16[1024,512]{1,0:T(8,128)(2,1)S(1)} custom-call(bf16[2,1024,512]{2,1,0:T(8,128)(2,1)S(1)} %get-tuple-element.18.parts_ref, bf16[4,128,128]{2,1,0:T(8,128)(2,1)S(1)} %bitcast.14, f32[4,128]{1,0:T(4,128)S(1)} %get-tuple-element.22.gain_ref), custom_call_target="tpu_custom_call" | custom-call | tf_op jit(solution)/shard_map/finish/pallas_call | solution.py:310
  50.5 21.7 %all_to_all.22.in_ref = bf16[8,128,512]{2,1,0:T(8,128)(2,1)S(1)} all-to-all(bf16[8,128,512]{2,1,0:T(8,128)(2,1)S(1)} %bitcast.10), channel_id=1, replica_groups={{4,5,6,7,0,1,2,3},{12,13,14,15,8,9,10,11},{20,21,22,23,16,17,18,19},{28..., dimensions={0} | all-to-all | bytes 2097152 | tf_op jit(solution)/shard_map/all_to_all | solution.py:319
  72.2 1.0 %lay_out.1 = bf16[128,4096]{1,0:T(8,128)(2,1)} custom-call(bf16[8,128,512]{2,1,0:T(8,128)(2,1)S(1)} %all_to_all.22.in_ref), custom_call_target="tpu_custom_call" | custom-call | tf_op jit(solution)/shard_map/lay_out/pallas_call | solution.py:321
Async XLA Ops:
  0.0 32.3 %copy-start = (bf16[1024,512]{1,0:T(8,128)(2,1)S(1)}, bf16[1024,512]{1,0:T(8,128)(2,1)}, u32[]{:S(2)}) copy-start(bf16[1024,512]{1,0:T(8,128)(2,1)} %key_ref.1) | copy-start | bytes 3145732
  0.0 32.3 %copy-start.2 = (f32[1024,4]{0,1:T(4,128)S(1)}, f32[1024,4]{0,1:T(4,128)}, u32[]{:S(2)}) copy-start(f32[1024,4]{0,1:T(4,128)} %param.8) | copy-start | bytes 49156
  0.0 32.3 %copy-start.4 = (f32[4096]{0:T(1024)S(1)}, f32[4096]{0:T(1024)}, u32[]{:S(2)}) copy-start(f32[4096]{0:T(1024)} %param.9) | copy-start | bytes 49156
  18.0 21.2 %all-to-all-start.1 = ((bf16[4,68,2,128]{3,2,1,0:T(2,128)(2,1)}), bf16[4,68,2,128]{3,2,1,0:T(2,128)(2,1)S(1)}, u32[]{:S(2)}, u32[]{:S(2)}) async-start(bf16[4,68,2,128]{3,2,1,0:T(2,128)(2,1)} %bitcast.3), calls=%async_computation.1 | async-start | bytes 278528 | tf_op jit(solution)/shard_map/all_to_all | solution.py:257
  32.4 1.2 %copy-start.1 = (bf16[1024,512]{1,0:T(8,128)(2,1)S(1)}, bf16[1024,512]{1,0:T(8,128)(2,1)}, u32[]{:S(2)}) copy-start(bf16[1024,512]{1,0:T(8,128)(2,1)} %value_ref.1) | copy-start | bytes 3145732
  33.6 1.2 %copy-start.3 = (bf16[1024,512]{1,0:T(8,128)(2,1)S(1)}, bf16[1024,512]{1,0:T(8,128)(2,1)}, u32[]{:S(2)}) copy-start(bf16[1024,512]{1,0:T(8,128)(2,1)} %query_ref.1) | copy-start | bytes 3145732

commit v6 on v5

--- a/solution.py
+++ b/solution.py
@@ -154,7 +154,6 @@
     parts_ref,
     gain_out_ref,
     place_out_ref,
-    total_ref,
 ):
     heads, tokens = rates_ref.shape
     size = query_ref.shape[1] // heads
@@ -173,26 +172,23 @@
         column = jnp.concatenate([columns[:, n : n + 1] for n in places], axis=0) - 0.5 * math.log2(size)
         row = jnp.concatenate([stacked[n : n + 1] for n in places], axis=1)
         parts_ref[0, :, at_h] = (query_ref[:, at_h].astype(F32) * jnp.exp2(column)).astype(BF16)
+        state = None
         for first in range(0, tokens, span):
-            at_s = slice(first, first + span)
-            scores = lax.dot_general(
-                query_ref[first:, at_h],
-                key_ref[at_s, at_h],
-                (((1,), (1,)), ((), ())),
-                preferred_element_type=F32,
-            )
-            weights = []
-            for start in range(first, tokens, span):
-                spread = column[start : start + span] - row[:, at_s]
-                if start == first:
-                    spread = jnp.where(place_t >= place_s, spread, -jnp.inf)
-                weights.append((scores[start - first : start - first + span] * jnp.exp2(spread)).astype(BF16))
-            part = jnp.dot(jnp.concatenate(weights, axis=0), value_ref[at_s, at_h], preferred_element_type=F32)
-            if first == 0:
-                total_ref[...] = part
-            else:
-                total_ref[first:, :] += part
-        parts_ref[1, :, at_h] = total_ref[...].astype(BF16)
+            at = slice(first, first + span)
+            query, key, value = query_ref[at, at_h], key_ref[at, at_h], value_ref[at, at_h]
+            scores = lax.dot_general(query, key, (((1,), (1,)), ((), ())), preferred_element_type=F32)
+            spread = jnp.where(place_t >= place_s, column[at] - row[:, at], -jnp.inf)
+            total = jnp.dot((scores * jnp.exp2(spread)).astype(BF16), value, preferred_element_type=F32)
+            if first > 0:
+                base = row[:, first - 1 : first]
+                scaled = (query.astype(F32) * jnp.exp2(column[at] - base)).astype(BF16)
+                total += jnp.dot(scaled, state.astype(BF16), preferred_element_type=F32)
+            if first + span < tokens:
+                end = row[:, first + span - 1 : first + span]
+                decayed = (key.T.astype(F32) * jnp.exp2(end - row[:, at])).astype(BF16)
+                added = jnp.dot(decayed, value, preferred_element_type=F32)
+                state = added if first == 0 else state * jnp.exp2(end - base) + added
+            parts_ref[1, at, at_h] = total.astype(BF16)
 
 
 def finish_kernel(span, first_row, parts_ref, incoming_ref, gain_ref, out_ref):
@@ -290,7 +286,6 @@
                 jax.ShapeDtypeStruct((heads, size), F32),
                 jax.ShapeDtypeStruct((1,), jnp.int32),
             ],
-            scratch_shapes=[pltpu.VMEM((tokens, size), F32)],
             compiler_params=pltpu.CompilerParams(vmem_limit_bytes=LARGE_VMEM),
             cost_estimate=pl.CostEstimate(
                 flops=3 * heads * tokens * tokens * size, bytes_accessed=12 * tokens * features, transcendentals=heads * tokens * tokens

time: 73.6 us -> 73.2 us (level)
  transfers between devices with their start and end apart: 1 -> 1, of which waited for: 0 -> 0; matrix products, arithmetic and copies ran while one was open for 0% -> 0% of each run, Pallas kernels for 6% -> 5%
where the time goes in v6:
time: 73.2 us; the launch traced here: 72.8 us
  blocking collectives  45.5 us (62%)
  starting transfers between devices  14.3 us (20%)
  Pallas kernels  10.4 us (14%)
  local copies, waits for them, and re-layouts  2.46 us (3%)
    all_to_all x2, blocking collectives, swap(): lax.all_to_all(sent, 'seq', 0, 0, tiled=True, axis_index_groups=groups)  23.8 us
    all_to_all x1, blocking collectives, per_device(): lax.all_to_all(sent, 'head', 0, 0, tiled=True, axis_index_groups=[head_or...  21.7 us
    all_to_all x1, starting transfers between devices, swap(): lax.all_to_all(sent, 'seq', 0, 0, tiled=True, axis_index_groups=groups)  14.3 us
    pallas_call x1, Pallas kernels, per_device(): pl.pallas_call(functools.partial(within_kernel, 256), in_specs=[in_smem]...  3.97 us
    pallas_call x1, Pallas kernels, per_device(): pl.pallas_call(summary_kernel, in_specs=[in_hbm] * 3, out_specs=in_vmem,...  2.95 us
    unnamed x10, local copies, waits for them, and re-layouts  2.46 us
  transfers between devices with their start and end apart: 1, of which 0 were waited for; matrix products, arithmetic and copies ran while one was open for 0% of the time, Pallas kernels for 5%

profile of v6, /device:TPU:1, one launch (start us, length us, event | category | flops | bytes accessed | tf_op | source)
XLA Modules:
  0.0 72.8 jit_solution(4016329267365590227)
XLA Ops:
  0.0 0.0 copy-start
  0.0 0.0 copy-start.2
  0.0 0.0 copy-start.4
  0.0 3.0 %summaries.1 = bf16[544,128]{1,0:T(8,128)(2,1)} custom-call(f32[4,1024]{1,0:T(4,128)} %bitcast.15, bf16[1024,512]{1,0:T(8,128)(2,1)} %key_ref.1, bf16[1024,512]{1,0:T(8,128)(2,1)} %value_ref.1), custom_call_target="tpu_custom_call" | custom-call | flops 134217728 | bytes 2097152 | tf_op jit(solution)/shard_map/summaries/pallas_call | solution.py:259
  3.0 14.3 %all_to_all.20 = bf16[16,17,2,128]{3,2,1,0:T(2,128)(2,1)S(1)} all-to-all(bf16[16,17,2,128]{3,2,1,0:T(2,128)(2,1)} %bitcast.18), channel_id=1, replica_groups={{264,272,280,256,392,400,408,384,136,144,152,128,8,16,24,0},{296,304,31..., dimensions={0} | all-to-all | bytes 278528 | tf_op jit(solution)/shard_map/all_to_all | solution.py:253
  17.2 0.7 group_totals.1
  18.0 14.3 %all-to-all-start.1 = ((bf16[4,68,2,128]{3,2,1,0:T(2,128)(2,1)}), bf16[4,68,2,128]{3,2,1,0:T(2,128)(2,1)S(1)}, u32[]{:S(2)}, u32[]{:S(2)}) async-start(bf16[4,68,2,128]{3,2,1,0:T(2,128)(2,1)} %bitcast.3), calls=%async_computation.1 | async-start | bytes 278528 | tf_op jit(solution)/shard_map/all_to_all | solution.py:253
  32.3 0.1 pad_add_fusion.place_ref
  32.3 0.0 copy-done
  32.3 0.0 copy-done.2
  32.4 0.0 copy-done.4
  32.4 0.0 copy-start.1
  32.4 1.2 %copy-done.1 = bf16[1024,512]{1,0:T(8,128)(2,1)S(1)} copy-done((bf16[1024,512]{1,0:T(8,128)(2,1)S(1)}, bf16[1024,512]{1,0:T(8,128)(2,1)}, u32[]{:S(2)}) %copy-start.1) | copy-done | bytes 1048600
  33.6 0.0 copy-start.3
  33.6 1.2 %copy-done.3 = bf16[1024,512]{1,0:T(8,128)(2,1)S(1)} copy-done((bf16[1024,512]{1,0:T(8,128)(2,1)S(1)}, bf16[1024,512]{1,0:T(8,128)(2,1)}, u32[]{:S(2)}) %copy-start.3) | copy-done | bytes 1048600
  34.8 4.0 %within.1 = (bf16[2,1024,512]{2,1,0:T(8,128)(2,1)S(1)}, f32[4,128]{1,0:T(4,128)S(1)}, s32[1]{0:T(128)}) custom-call(s32[2]{0:T(128)S(1)} %pad_add_fusion.place_ref, f32[32,128]{1,0:T(8,128)S(1)} %bitcast.17, f32[4,1024]{1,0:T(4,128)S(1)} %bitcast.16, bf16[1024,512]{1,0:T(8,128)(2,1)S(1)} %copy-done.3, bf16[1024,512]{1,0:T(8,128)(2,1)S(1)} %copy-done, ...), custom_call_target="tpu_custom_call" | custom-call | flops 1610612736 | bytes 6291456 | tf_op jit(solution)/shard_map/within/pallas_call | solution.py:280
  38.8 0.0 all-to-all-done.1
  38.8 0.7 carry.1
  39.5 9.6 %all_to_all.21 = bf16[16,32,128]{2,1,0:T(8,128)(2,1)S(1)} all-to-all(bf16[16,32,128]{2,1,0:T(8,128)(2,1)S(1)} %carry.1), channel_id=1, replica_groups={{264,272,280,256,392,400,408,384,136,144,152,128,8,16,24,0},{296,304,31..., dimensions={0} | all-to-all | bytes 262144 | tf_op jit(solution)/shard_map/all_to_all | solution.py:253
  49.0 1.1 %finish.1 = bf16[1024,512]{1,0:T(8,128)(2,1)S(1)} custom-call(bf16[2,1024,512]{2,1,0:T(8,128)(2,1)S(1)} %get-tuple-element.18.parts_ref, bf16[4,128,128]{2,1,0:T(8,128)(2,1)S(1)} %bitcast.14, f32[4,128]{1,0:T(4,128)S(1)} %get-tuple-element.22.gain_ref), custom_call_target="tpu_custom_call" | custom-call | tf_op jit(solution)/shard_map/finish/pallas_call | solution.py:305
  50.1 21.7 %all_to_all.22.in_ref = bf16[8,128,512]{2,1,0:T(8,128)(2,1)S(1)} all-to-all(bf16[8,128,512]{2,1,0:T(8,128)(2,1)S(1)} %bitcast.10), channel_id=1, replica_groups={{4,5,6,7,0,1,2,3},{12,13,14,15,8,9,10,11},{20,21,22,23,16,17,18,19},{28..., dimensions={0} | all-to-all | bytes 2097152 | tf_op jit(solution)/shard_map/all_to_all | solution.py:314
  71.7 1.0 %lay_out.1 = bf16[128,4096]{1,0:T(8,128)(2,1)} custom-call(bf16[8,128,512]{2,1,0:T(8,128)(2,1)S(1)} %all_to_all.22.in_ref), custom_call_target="tpu_custom_call" | custom-call | tf_op jit(solution)/shard_map/lay_out/pallas_call | solution.py:316
Async XLA Ops:
  0.0 32.3 %copy-start = (bf16[1024,512]{1,0:T(8,128)(2,1)S(1)}, bf16[1024,512]{1,0:T(8,128)(2,1)}, u32[]{:S(2)}) copy-start(bf16[1024,512]{1,0:T(8,128)(2,1)} %key_ref.1) | copy-start | bytes 3145732
  0.0 32.3 %copy-start.2 = (f32[1024,4]{0,1:T(4,128)S(1)}, f32[1024,4]{0,1:T(4,128)}, u32[]{:S(2)}) copy-start(f32[1024,4]{0,1:T(4,128)} %param.8) | copy-start | bytes 49156
  0.0 32.3 %copy-start.4 = (f32[4096]{0:T(1024)S(1)}, f32[4096]{0:T(1024)}, u32[]{:S(2)}) copy-start(f32[4096]{0:T(1024)} %param.9) | copy-start | bytes 49156
  18.0 20.8 %all-to-all-start.1 = ((bf16[4,68,2,128]{3,2,1,0:T(2,128)(2,1)}), bf16[4,68,2,128]{3,2,1,0:T(2,128)(2,1)S(1)}, u32[]{:S(2)}, u32[]{:S(2)}) async-start(bf16[4,68,2,128]{3,2,1,0:T(2,128)(2,1)} %bitcast.3), calls=%async_computation.1 | async-start | bytes 278528 | tf_op jit(solution)/shard_map/all_to_all | solution.py:253
  32.4 1.2 %copy-start.1 = (bf16[1024,512]{1,0:T(8,128)(2,1)S(1)}, bf16[1024,512]{1,0:T(8,128)(2,1)}, u32[]{:S(2)}) copy-start(bf16[1024,512]{1,0:T(8,128)(2,1)} %value_ref.1) | copy-start | bytes 3145732
  33.6 1.2 %copy-start.3 = (bf16[1024,512]{1,0:T(8,128)(2,1)S(1)}, bf16[1024,512]{1,0:T(8,128)(2,1)}, u32[]{:S(2)}) copy-start(bf16[1024,512]{1,0:T(8,128)(2,1)} %query_ref.1) | copy-start | bytes 3145732

commit v7 on v6

--- a/solution.py
+++ b/solution.py
@@ -13,7 +13,7 @@
 BF16 = jnp.bfloat16
 PARTS = 2
 QUAD = 4
-NEAR = [1, 2, 3, 0]
+NEAR = [2, 1, 3, 0]
 FAR = [2, 3, 1, 0]
 ROWS = [2, 3, 1, 0]
 FIRST_HEAD = 4

time: 73.2 us -> 73.1 us (level)
    all_to_all x2, blocking collectives: 23.8 us -> 22.8 us  [swap(): lax.all_to_all(sent, 'seq', 0, 0, tiled=True, axis_index_groups=groups)]
where the time goes in v7:
time: 73.1 us; the launch traced here: 72.7 us
  blocking collectives  44.8 us (61%)
  starting transfers between devices  14.9 us (20%)
  Pallas kernels  10.4 us (14%)
  local copies, waits for them, and re-layouts  2.46 us (3%)
    all_to_all x2, blocking collectives, swap(): lax.all_to_all(sent, 'seq', 0, 0, tiled=True, axis_index_groups=groups)  22.8 us
    all_to_all x1, blocking collectives, per_device(): lax.all_to_all(sent, 'head', 0, 0, tiled=True, axis_index_groups=[head_or...  22 us
    all_to_all x1, starting transfers between devices, swap(): lax.all_to_all(sent, 'seq', 0, 0, tiled=True, axis_index_groups=groups)  14.9 us
    pallas_call x1, Pallas kernels, per_device(): pl.pallas_call(functools.partial(within_kernel, 256), in_specs=[in_smem]...  3.97 us
    pallas_call x1, Pallas kernels, per_device(): pl.pallas_call(summary_kernel, in_specs=[in_hbm] * 3, out_specs=in_vmem,...  2.95 us
    unnamed x10, local copies, waits for them, and re-layouts  2.46 us
  transfers between devices with their start and end apart: 1, of which 0 were waited for; matrix products, arithmetic and copies ran while one was open for 0% of the time, Pallas kernels for 5%

profile of v7, /device:TPU:1, one launch (start us, length us, event | category | flops | bytes accessed | tf_op | source)
XLA Modules:
  0.0 72.7 jit_solution(11738857097592427122)
XLA Ops:
  0.0 0.0 copy-start
  0.0 0.0 copy-start.2
  0.0 0.0 copy-start.4
  0.0 3.0 %summaries.1 = bf16[544,128]{1,0:T(8,128)(2,1)} custom-call(f32[4,1024]{1,0:T(4,128)} %bitcast.15, bf16[1024,512]{1,0:T(8,128)(2,1)} %key_ref.1, bf16[1024,512]{1,0:T(8,128)(2,1)} %value_ref.1), custom_call_target="tpu_custom_call" | custom-call | flops 134217728 | bytes 2097152 | tf_op jit(solution)/shard_map/summaries/pallas_call | solution.py:259
  3.0 13.4 %all_to_all.20 = bf16[16,17,2,128]{3,2,1,0:T(2,128)(2,1)S(1)} all-to-all(bf16[16,17,2,128]{3,2,1,0:T(2,128)(2,1)} %bitcast.18), channel_id=1, replica_groups={{272,264,280,256,400,392,408,384,144,136,152,128,16,8,24,0},{304,296,31..., dimensions={0} | all-to-all | bytes 278528 | tf_op jit(solution)/shard_map/all_to_all | solution.py:253
  16.3 0.7 group_totals.1
  17.1 14.9 %all-to-all-start.1 = ((bf16[4,68,2,128]{3,2,1,0:T(2,128)(2,1)}), bf16[4,68,2,128]{3,2,1,0:T(2,128)(2,1)S(1)}, u32[]{:S(2)}, u32[]{:S(2)}) async-start(bf16[4,68,2,128]{3,2,1,0:T(2,128)(2,1)} %bitcast.3), calls=%async_computation.1 | async-start | bytes 278528 | tf_op jit(solution)/shard_map/all_to_all | solution.py:253
  31.9 0.1 pad_add_fusion.place_ref
  32.0 0.0 copy-done
  32.0 0.0 copy-done.2
  32.0 0.0 copy-done.4
  32.0 0.0 copy-start.1
  32.0 1.2 %copy-done.1 = bf16[1024,512]{1,0:T(8,128)(2,1)S(1)} copy-done((bf16[1024,512]{1,0:T(8,128)(2,1)S(1)}, bf16[1024,512]{1,0:T(8,128)(2,1)}, u32[]{:S(2)}) %copy-start.1) | copy-done | bytes 1048600
  33.2 0.0 copy-start.3
  33.3 1.2 %copy-done.3 = bf16[1024,512]{1,0:T(8,128)(2,1)S(1)} copy-done((bf16[1024,512]{1,0:T(8,128)(2,1)S(1)}, bf16[1024,512]{1,0:T(8,128)(2,1)}, u32[]{:S(2)}) %copy-start.3) | copy-done | bytes 1048600
  34.5 4.0 %within.1 = (bf16[2,1024,512]{2,1,0:T(8,128)(2,1)S(1)}, f32[4,128]{1,0:T(4,128)S(1)}, s32[1]{0:T(128)}) custom-call(s32[2]{0:T(128)S(1)} %pad_add_fusion.place_ref, f32[32,128]{1,0:T(8,128)S(1)} %bitcast.17, f32[4,1024]{1,0:T(4,128)S(1)} %bitcast.16, bf16[1024,512]{1,0:T(8,128)(2,1)S(1)} %copy-done.3, bf16[1024,512]{1,0:T(8,128)(2,1)S(1)} %copy-done, ...), custom_call_target="tpu_custom_call" | custom-call | flops 1610612736 | bytes 6291456 | tf_op jit(solution)/shard_map/within/pallas_call | solution.py:280
  38.5 0.0 all-to-all-done.1
  38.5 0.7 carry.1
  39.1 9.5 %all_to_all.21 = bf16[16,32,128]{2,1,0:T(8,128)(2,1)S(1)} all-to-all(bf16[16,32,128]{2,1,0:T(8,128)(2,1)S(1)} %carry.1), channel_id=1, replica_groups={{272,264,280,256,400,392,408,384,144,136,152,128,16,8,24,0},{304,296,31..., dimensions={0} | all-to-all | bytes 262144 | tf_op jit(solution)/shard_map/all_to_all | solution.py:253
  48.6 1.1 %finish.1 = bf16[1024,512]{1,0:T(8,128)(2,1)S(1)} custom-call(bf16[2,1024,512]{2,1,0:T(8,128)(2,1)S(1)} %get-tuple-element.18.parts_ref, bf16[4,128,128]{2,1,0:T(8,128)(2,1)S(1)} %bitcast.14, f32[4,128]{1,0:T(4,128)S(1)} %get-tuple-element.22.gain_ref), custom_call_target="tpu_custom_call" | custom-call | tf_op jit(solution)/shard_map/finish/pallas_call | solution.py:305
  49.7 22.0 %all_to_all.22.in_ref = bf16[8,128,512]{2,1,0:T(8,128)(2,1)S(1)} all-to-all(bf16[8,128,512]{2,1,0:T(8,128)(2,1)S(1)} %bitcast.10), channel_id=1, replica_groups={{4,5,6,7,0,1,2,3},{12,13,14,15,8,9,10,11},{20,21,22,23,16,17,18,19},{28..., dimensions={0} | all-to-all | bytes 2097152 | tf_op jit(solution)/shard_map/all_to_all | solution.py:314
  71.6 1.0 %lay_out.1 = bf16[128,4096]{1,0:T(8,128)(2,1)} custom-call(bf16[8,128,512]{2,1,0:T(8,128)(2,1)S(1)} %all_to_all.22.in_ref), custom_call_target="tpu_custom_call" | custom-call | tf_op jit(solution)/shard_map/lay_out/pallas_call | solution.py:316
Async XLA Ops:
  0.0 32.0 %copy-start = (bf16[1024,512]{1,0:T(8,128)(2,1)S(1)}, bf16[1024,512]{1,0:T(8,128)(2,1)}, u32[]{:S(2)}) copy-start(bf16[1024,512]{1,0:T(8,128)(2,1)} %key_ref.1) | copy-start | bytes 3145732
  0.0 32.0 %copy-start.2 = (f32[1024,4]{0,1:T(4,128)S(1)}, f32[1024,4]{0,1:T(4,128)}, u32[]{:S(2)}) copy-start(f32[1024,4]{0,1:T(4,128)} %param.8) | copy-start | bytes 49156
  0.0 32.0 %copy-start.4 = (f32[4096]{0:T(1024)S(1)}, f32[4096]{0:T(1024)}, u32[]{:S(2)}) copy-start(f32[4096]{0:T(1024)} %param.9) | copy-start | bytes 49156
  17.1 21.4 %all-to-all-start.1 = ((bf16[4,68,2,128]{3,2,1,0:T(2,128)(2,1)}), bf16[4,68,2,128]{3,2,1,0:T(2,128)(2,1)S(1)}, u32[]{:S(2)}, u32[]{:S(2)}) async-start(bf16[4,68,2,128]{3,2,1,0:T(2,128)(2,1)} %bitcast.3), calls=%async_computation.1 | async-start | bytes 278528 | tf_op jit(solution)/shard_map/all_to_all | solution.py:253
  32.0 1.2 %copy-start.1 = (bf16[1024,512]{1,0:T(8,128)(2,1)S(1)}, bf16[1024,512]{1,0:T(8,128)(2,1)}, u32[]{:S(2)}) copy-start(bf16[1024,512]{1,0:T(8,128)(2,1)} %value_ref.1) | copy-start | bytes 3145732
  33.2 1.2 %copy-start.3 = (bf16[1024,512]{1,0:T(8,128)(2,1)S(1)}, bf16[1024,512]{1,0:T(8,128)(2,1)}, u32[]{:S(2)}) copy-start(bf16[1024,512]{1,0:T(8,128)(2,1)} %query_ref.1) | copy-start | bytes 3145732
